TPU v7x, 128 devices: a whole 4x4x4 slice. The times are simulated.
128 devices in a mesh: expert: 16 (over z, y), tensor: 8 (over x, core).
Axes of the slice: x: 4, y: 4, z: 4, core: 2. Of those that a mesh axis runs over, the one named last changes fastest.
Arguments:
- tokens: bfloat16 [6144, 2048], P('expert'), may hold values from -6 to 6
- out_grad: bfloat16 [6144, 2048], P('expert'), may hold values from -6 to 6
- routes: int32 [6144, 6], P('expert'), may hold values from 0 to 63, all different within a row; in each aligned block of 384 rows (0 to 383, 384 to 767, ...) at most 48 rows name the same one
- segment: int32 [6144], replicated, may hold values from 0 to 2, as said below
- norm_gain: float32 [2048], replicated, may hold values from 0.5 to 1.5
- q_weight: bfloat16 [2048, 3072], P(None, 'tensor'), may hold values from -0.125 to 0.125
- kv_down: bfloat16 [2048, 576], replicated, may hold values from -0.125 to 0.125
- kv_gain: float32 [512], replicated, may hold values from 0.5 to 1.5
- kv_up: bfloat16 [512, 4096], P(None, 'tensor'), may hold values from -0.25 to 0.25
- out_weight: bfloat16 [2048, 2048], P('tensor'), may hold values from -1.5 to 1.5
- mix_gain: float32 [2048], replicated, may hold values from 0.5 to 1.5
- router: bfloat16 [2048, 64], replicated, may hold values from -0.0625 to 0.0625
- shared_gate: bfloat16 [2048, 2816], P(None, 'tensor'), may hold values from -0.125 to 0.125
- shared_up: bfloat16 [2048, 2816], P(None, 'tensor'), may hold values from -0.125 to 0.125
- shared_down: bfloat16 [2816, 2048], P('tensor'), may hold values from -0.15625 to 0.15625
- expert_gate: bfloat16 [64, 2048, 1408], P('expert', None, 'tensor'), may hold values from -0.125 to 0.125
- expert_up: bfloat16 [64, 2048, 1408], P('expert', None, 'tensor'), may hold values from -0.125 to 0.125
- expert_down: bfloat16 [64, 1408, 2048], P('expert', 'tensor'), may hold values from -6 to 6
- step_size: float32 [1], replicated, may hold values from 0.0001 to 0.001
- threshold: float32 [1], replicated, may hold values from 0.5 to 2
Outputs:
- layer_out: bfloat16 [6144, 2048], P('expert')
- tokens_grad: float32 [6144, 2048], P('expert')
- q_weight_grad: float32 [2048, 3072], P('expert', 'tensor')
- kv_down_grad: float32 [2048, 576], P('expert')
- kv_up_grad: float32 [512, 4096], P('expert', 'tensor')
- out_weight_grad: float32 [2048, 2048], P('tensor', 'expert')
- router_grad: float32 [2048, 64], P('expert')
- norm_gain_grad: float32 [2048], P('expert')
- kv_gain_grad: float32 [512], P('expert')
- mix_gain_grad: float32 [2048], P('expert')
- shared_gate_grad: float32 [2048, 2816], P('expert', 'tensor')
- shared_up_grad: float32 [2048, 2816], P('expert', 'tensor')
- shared_down_grad: float32 [2816, 2048], P('tensor', 'expert')
- expert_gate_grad: float32 [64, 2048, 1408], P('expert', None, 'tensor')
- expert_up_grad: float32 [64, 2048, 1408], P('expert', None, 'tensor')
- expert_down_grad: float32 [64, 1408, 2048], P('expert', 'tensor')
- q_weight_new: float32 [2048, 3072], P('expert', 'tensor')
- kv_up_new: float32 [512, 4096], P('expert', 'tensor')
Inputs may be any that keep to these rules, and one draw needn't show every extreme that they name: `routes`: each row names 6 different experts. In the rows of one index of the expert axis (384 aligned rows) no expert is named by more than 48 rows, a bound that some block reaches. In each group continuations 1 to 2 come first in order, each 128 tokens or more, 512 tokens together; the last 1024 tokens have segment 0.
All inputs are finite; a program needn't handle non-finite values.
Results may differ from a plain program's by a relative error of at most 0.019.
Values may be sent and summed in bfloat16 or wider, within the bound.
No kernel may reach another device: no remote copies, remote signals or barrier semaphores. Data moves between devices by JAX's collectives and lax.ppermute only.
A program may use at most 384 MiB of HBM per device.

v0:
```python
import functools
import math

import jax
import jax.numpy as jnp
from jax import lax
from jax.experimental import pallas as pl
from jax.experimental.pallas import tpu as pltpu
from jax.sharding import Mesh
from jax.sharding import PartitionSpec as P

D = 2048
HALF = D // 2
NOPE = 128
ROPE = 64
VDIM = 128
KVRANK = 512
TOPK = 6
PROMPT = 1024
CONT = 2
EXPERTS = 64
CAP = 48
SPAN = 4
RING = 4
OWN = 48
EPSILON = 1e-06

BF = jnp.bfloat16
F32 = jnp.float32
EXPERT = ("z", "y")
TENSOR = ("x", "c")


def dot(left, right, contract=((1,), (0,))):
    return lax.dot_general(left, right, (contract, ((), ())), preferred_element_type=F32)


def swap(block):
    return lax.ppermute(block, "c", [(0, 1), (1, 0)])


def shift(block, axis, step):
    return lax.ppermute(block, axis, [(i, (i + step) % RING) for i in range(RING)])


def spread(block):
    return lax.all_to_all(block, EXPERT, split_axis=0, concat_axis=0, tiled=True)


def pick_index(blocks, index, axis=0):
    return lax.dynamic_index_in_dim(blocks, index, axis, keepdims=False)


def sum_ring(blocks, axis, index):
    return sum_sent(*ring_parts(blocks, index), axis)


def ring_parts(blocks, index):
    own = pick_index(blocks, index)
    return own, [pick_index(blocks, (index + step) % RING).astype(BF) for step in (1, 2, 3)]


def sum_sent(own, parts, axis):
    for step in (1, 2, 3):
        own = own + shift(parts[step - 1], axis, step).astype(F32)
    return own


def gather_ring(block, axis, index):
    blocks = jnp.zeros((RING,) + block.shape, block.dtype)
    blocks = lax.dynamic_update_index_in_dim(blocks, block, index, 0)
    for step in (1, 2, 3):
        blocks = lax.dynamic_update_index_in_dim(
            blocks, shift(block, axis, step), (index - step) % RING, 0
        )
    return blocks


def gather_pair(block, core):
    blocks = jnp.zeros((2,) + block.shape, block.dtype)
    blocks = lax.dynamic_update_index_in_dim(blocks, block, core, 0)
    return lax.dynamic_update_index_in_dim(blocks, swap(block), 1 - core, 0)


def gather_rows(block):
    return lax.all_gather(block, TENSOR, axis=0, tiled=True)


def after(value, *others):
    return lax.optimization_barrier((value, *others))[0]


PIECE = 176
HIDDEN = RING * PIECE
SLOTS = 16 * CAP
TILE = 256
EXTRA = 128
NT = ((1,), (1,))
TN = ((0,), (0,))
VMEM_LIMIT = 56 << 20
HINT = 64


def whole(*shape):
    return pl.BlockSpec(shape, lambda *_: (0,) * len(shape))


def anywhere():
    return pl.BlockSpec(memory_space=pl.ANY)


def copy_all(pairs, sems):
    copies = [pltpu.make_async_copy(a, b, sems.at[i]) for i, (a, b) in enumerate(pairs)]
    for one in copies:
        one.start()
    for one in copies:
        one.wait()


def cost(flops, bytes_accessed, exps=0):
    return pl.CostEstimate(
        flops=int(flops) // HINT, bytes_accessed=int(bytes_accessed) // HINT, transcendentals=0
    )


OUTWARD = (208, 320)
HOMEWARD = (96, 112, 80, 240)


def spans(parts):
    found, start = [], 0
    for part, size in enumerate(parts):
        at = start
        while at < start + size:
            weight, inside = divmod(at, PIECE)
            length = min(PIECE - inside, start + size - at)
            found.append((part, at - start, weight, inside, length))
            at += length
        start += size
    return found


def pack_kernel(x_ref, *refs):
    for step in range(3):
        for part, at, weight, inside, length in spans(OUTWARD):
            out = refs[9 + step * len(OUTWARD) + part]
            out[at : at + length, :] = refs[3 * step + weight][0, inside : inside + length, :]


def pack(x, gate, up, down):
    block = 512

    def source(step):
        return pl.BlockSpec((1, PIECE, block), lambda i, x: (lax.rem(x[0] + step, RING), 0, i))

    outs = pl.pallas_call(
        pack_kernel,
        grid_spec=pltpu.PrefetchScalarGridSpec(
            num_scalar_prefetch=1,
            grid=(D // block,),
            in_specs=[source(step) for step in (1, 2, 3) for _ in range(3)],
            out_specs=[pl.BlockSpec((size, block), lambda i, _: (0, i)) for size in OUTWARD] * 3,
        ),
        out_shape=[jax.ShapeDtypeStruct((size, D), BF) for size in OUTWARD] * 3,
        compiler_params=pltpu.CompilerParams(vmem_limit_bytes=VMEM_LIMIT),
        cost_estimate=cost(0, 13 << 20),
        name="pack_weights",
    )(x.reshape(1), *((gate, up, down) * 3))
    return [outs[part :: len(OUTWARD)] for part in range(len(OUTWARD))]


def unpack_kernel(x_ref, *refs):
    outs = refs[len(HOMEWARD) * RING :]
    for step in range(RING):
        index = lax.rem(x_ref[0] + step, RING)
        for part, at, weight, inside, length in spans(HOMEWARD):
            piece = refs[part * RING + step]
            outs[weight][index, inside : inside + length, :] = piece[at : at + length, :].astype(F32)


def unpack(x, parts):
    block = 512
    return pl.pallas_call(
        unpack_kernel,
        grid_spec=pltpu.PrefetchScalarGridSpec(
            num_scalar_prefetch=1,
            grid=(D // block,),
            in_specs=[
                pl.BlockSpec((size, block), lambda i, _: (0, i))
                for size in HOMEWARD
                for _ in range(RING)
            ],
            out_specs=[pl.BlockSpec((RING, PIECE, block), lambda i, _: (0, 0, i))] * 3,
        ),
        out_shape=[jax.ShapeDtypeStruct((RING, PIECE, D), F32)] * 3,
        compiler_params=pltpu.CompilerParams(vmem_limit_bytes=VMEM_LIMIT),
        cost_estimate=cost(0, 26 << 20),
        name="unpack_gradients",
    )(x.reshape(1), *[piece for part in parts for piece in part])


def load_weight(which, index, own_ref, parts, weight):
    pairs = [(own_ref.at[index], weight.at[pl.ds(0, PIECE)])]
    for part, at, kind, inside, length in spans(OUTWARD):
        if kind == which:
            for step, piece in enumerate(parts[part]):
                start = (step + 1) * PIECE + inside
                pairs.append((piece.at[pl.ds(at, length)], weight.at[pl.ds(start, length)]))
    return pairs


def halves_of(place_ref):
    core = place_ref[1]
    return (
        pl.ds(pl.multiple_of(core * HALF, HALF), HALF),
        pl.ds(pl.multiple_of((1 - core) * HALF, HALF), HALF),
    )


def expert_kernel(
    place_ref,
    mine_ref,
    other_ref,
    grad_mine_ref,
    grad_other_ref,
    gate_ref,
    own_gate,
    own_up,
    own_down,
    p1,
    p2,
    p3,
    q1,
    q2,
    q3,
    act_ref,
    scaled_ref,
    gate_grad_ref,
    up_grad_ref,
    keep_ref,
    give_ref,
    columns_ref,
    gate_w,
    up_w,
    down_w,
    sems,
):
    @pl.when(pl.program_id(0) == 0)
    def _():
        index = place_ref[0]
        parts = {0: (p1, p2, p3), 1: (q1, q2, q3)}
        copy_all(
            load_weight(0, index, own_gate, parts, gate_w)
            + load_weight(1, index, own_up, parts, up_w)
            + load_weight(2, index, own_down, parts, down_w),
            sems,
        )

    first, second = halves_of(place_ref)
    mine, other = mine_ref[...], other_ref[...]
    extra = gate_ref[...].astype(F32)
    gate = extra[:, 0:1] + extra[:, 1:2]
    gate_lin = dot(mine, gate_w[:, first], NT) + dot(other, gate_w[:, second], NT)
    up_lin = dot(mine, up_w[:, first], NT) + dot(other, up_w[:, second], NT)
    raw = dot(grad_mine_ref[...], down_w[:, first], NT)
    raw = raw + dot(grad_other_ref[...], down_w[:, second], NT)
    sigmoid = jax.nn.sigmoid(gate_lin)
    silu = gate_lin * sigmoid
    act = (silu * up_lin).astype(BF)
    act_ref[...] = act
    act = act.astype(F32)
    scaled_ref[...] = (act * gate).astype(BF)
    act_grad = raw * gate
    gate_grad = (act_grad * up_lin * (sigmoid * (1.0 + gate_lin * (1.0 - sigmoid)))).astype(BF)
    up_grad = (act_grad * silu).astype(BF)
    gate_grad_ref[...] = gate_grad
    up_grad_ref[...] = up_grad
    keep_ref[...] = dot(gate_grad, gate_w[:, first]) + dot(up_grad, up_w[:, first])
    give_ref[...] = (dot(gate_grad, gate_w[:, second]) + dot(up_grad, up_w[:, second])).astype(BF)
    slot_grad = jnp.sum(act * raw, axis=1, keepdims=True)
    high = slot_grad.astype(BF).astype(F32)
    lane = lax.broadcasted_iota(jnp.int32, (TILE, EXTRA), 1)
    expert_id = place_ref[2]
    columns_ref[...] = jnp.where(
        lane == expert_id, high, jnp.where(lane == EXPERTS + expert_id, slot_grad - high, 0.0)
    ).astype(BF)


def expert_pass(place, mine, other, gate, up, down, packed):
    rows = lambda width, at=0: pl.BlockSpec((TILE, width), lambda i, _: (i, at))
    shape = lambda width, dtype: jax.ShapeDtypeStruct((SLOTS, width), dtype)
    return pl.pallas_call(
        expert_kernel,
        grid_spec=pltpu.PrefetchScalarGridSpec(
            num_scalar_prefetch=1,
            grid=(SLOTS // TILE,),
            in_specs=[rows(HALF)] * 2 + [rows(HALF, 1)] * 2 + [rows(EXTRA, D // EXTRA)]
            + [anywhere()] * 9,
            out_specs=[rows(HIDDEN)] * 4 + [rows(HALF)] * 2 + [rows(EXTRA)],
            scratch_shapes=[pltpu.VMEM((HIDDEN, D), BF)] * 3 + [pltpu.SemaphoreType.DMA((15,))],
        ),
        out_shape=[shape(HIDDEN, BF)] * 4
        + [shape(HALF, F32), shape(HALF, BF), shape(EXTRA, BF)],
        compiler_params=pltpu.CompilerParams(vmem_limit_bytes=VMEM_LIMIT),
        cost_estimate=cost(10 * SLOTS * D * HIDDEN, 24 << 20, SLOTS * HIDDEN),
        name="expert_pass",
    )(place, mine, other, mine, other, mine, gate, up, down, *[p for part in packed for p in part])


def produce_kernel(place_ref, act_ref, mine_ref, own_down, p1, p2, p3, keep_ref, give_ref, down, sems):
    @pl.when(pl.program_id(0) == 0)
    def _():
        copy_all(load_weight(2, place_ref[0], own_down, {1: (p1, p2, p3)}, down), sems)

    first, second = halves_of(place_ref)
    extra = mine_ref[...].astype(F32)
    gate = extra[:, 0:1] + extra[:, 1:2]
    keep_ref[...] = dot(act_ref[...], down[:, first]) * gate
    give_ref[...] = (dot(act_ref[...], down[:, second]) * gate).astype(BF)


def produce(place, act, mine, down, packed):
    rows = lambda width: pl.BlockSpec((TILE, width), lambda i, _: (i, 0))
    return pl.pallas_call(
        produce_kernel,
        grid_spec=pltpu.PrefetchScalarGridSpec(
            num_scalar_prefetch=1,
            grid=(SLOTS // TILE,),
            in_specs=[
                rows(HIDDEN),
                pl.BlockSpec((TILE, EXTRA), lambda i, _: (i, D // EXTRA)),
            ]
            + [anywhere()] * 4,
            out_specs=[rows(HALF)] * 2,
            scratch_shapes=[pltpu.VMEM((HIDDEN, D), BF), pltpu.SemaphoreType.DMA((4,))],
        ),
        out_shape=[
            jax.ShapeDtypeStruct((SLOTS, HALF), F32),
            jax.ShapeDtypeStruct((SLOTS, HALF), BF),
        ],
        compiler_params=pltpu.CompilerParams(vmem_limit_bytes=VMEM_LIMIT),
        cost_estimate=cost(2 * SLOTS * D * HIDDEN, 9 << 20),
        name="produce",
    )(place, act, mine, down, *packed[1])


def weight_grad_kernel(place_ref, *refs, weights, parts):
    lefts = refs[: len(weights)]
    rights, outs = refs[len(weights) : -len(parts) * RING], refs[-len(parts) * RING :]
    own = pl.program_id(0) < 2
    rights = [jnp.where(own, rights[i][...], rights[i + 1][...]) for i in range(0, len(rights), 2)]
    for left, weight in zip(lefts, weights):
        right = rights[1] if weight == 2 and len(rights) > 1 else rights[0]
        product = dot(left[...], right, TN).astype(BF)
        for step in range(RING):
            for part, at, kind, inside, length in spans(HOMEWARD):
                if kind == weight:
                    start = step * PIECE + inside
                    out = outs[parts.index(part) * RING + step]
                    out[at : at + length, :] = product[start : start + length, :]


def weight_grads(place, weights, parts, lefts, rows):
    block = HALF // 2
    mine = [pl.BlockSpec((SLOTS, block), lambda i, _, at=at: (0, at + jnp.minimum(i, 1))) for at in (0, 2)]
    other = [
        pl.BlockSpec((SLOTS, block), lambda i, _, at=at: (0, at + jnp.maximum(i - 2, 0)))
        for at in (0, 2)
    ]
    sizes = [HOMEWARD[part] for part in parts for _ in range(RING)]
    outs = pl.pallas_call(
        functools.partial(weight_grad_kernel, weights=weights, parts=parts),
        grid_spec=pltpu.PrefetchScalarGridSpec(
            num_scalar_prefetch=1,
            grid=(4,),
            in_specs=[whole(SLOTS, HIDDEN)] * len(lefts)
            + [mine[0], other[0], mine[1], other[1]],
            out_specs=[
                pl.BlockSpec((size, block), lambda i, place: (0, lax.rem(2 * place[1] + i, 4)))
                for size in sizes
            ],
        ),
        out_shape=[jax.ShapeDtypeStruct((size, D), BF) for size in sizes],
        compiler_params=pltpu.CompilerParams(vmem_limit_bytes=VMEM_LIMIT),
        cost_estimate=cost(2 * len(lefts) * SLOTS * D * HIDDEN, 18 << 20),
        name="weight_grads",
    )(place, *lefts, *rows, *rows)
    return [outs[i * RING : (i + 1) * RING] for i in range(len(parts))]


SHARED = 352
WIDE = 384
ATT = 2 * VDIM


def shared_kernel(mixed, out_grad, gate_w, up_w, down_w, part, mixed_grad, grads):
    gate_lin = dot(mixed[...], gate_w[...], NT)
    up_lin = dot(mixed[...], up_w[...], NT)
    sigmoid = jax.nn.sigmoid(gate_lin)
    silu = gate_lin * sigmoid
    act = (silu * up_lin).astype(BF)
    act_grad = dot(out_grad[...], down_w[...], NT)
    gate_grad = (act_grad * up_lin * (sigmoid * (1.0 + gate_lin * (1.0 - sigmoid)))).astype(BF)
    up_grad = (act_grad * silu).astype(BF)
    for start in range(0, D, 512):
        at = slice(start, start + 512)
        part[:, at] = dot(act, down_w[:, at])
        mixed_grad[:, at] = dot(gate_grad, gate_w[:, at]) + dot(up_grad, up_w[:, at])
        zeros = jnp.zeros((512, WIDE - SHARED), BF)
        for i, (left, right) in enumerate(((mixed, gate_grad), (mixed, up_grad), (out_grad, act))):
            start = i * WIDE
            grads[at, start : start + SHARED] = dot(left[:, at], right, TN).astype(BF)
            grads[at, start + SHARED : start + WIDE] = zeros


def shared_experts(mixed, out_grad, gate_w, up_w, down_w):
    args = (mixed, out_grad, gate_w, up_w, down_w)
    rows = mixed.shape[0]
    outs = [
        jax.ShapeDtypeStruct((rows, D), F32),
        jax.ShapeDtypeStruct((rows, D), F32),
        jax.ShapeDtypeStruct((D, 3 * WIDE), BF),
    ]
    return pl.pallas_call(
        shared_kernel,
        grid=(1,),
        in_specs=[whole(*arg.shape) for arg in args],
        out_specs=[whole(*out.shape) for out in outs],
        out_shape=outs,
        compiler_params=pltpu.CompilerParams(vmem_limit_bytes=VMEM_LIMIT),
        cost_estimate=cost(18 * rows * D * SHARED, 18 << 20, rows * SHARED),
        name="shared_experts",
    )(*args)


GROUP = 1536
ROWS = 384
LATENT = KVRANK + ROPE
HEADS = 2
HEAD = NOPE + ROPE
SCALE = 1.0 / math.sqrt(HEAD)


def turn(block, cosine, sine):
    half = ROPE // 2
    return block * cosine + jnp.concatenate([block[:, half:], block[:, :half]], axis=1) * sine


def mask_bias(seg_keys, seg_rows, row_start):
    key = lax.broadcasted_iota(jnp.int32, (GROUP, ROWS), 0)
    row = lax.broadcasted_iota(jnp.int32, (GROUP, ROWS), 1) + row_start
    same = (seg_keys == seg_rows) & (key <= row)
    return jnp.where(same | ((seg_keys == 0) & (seg_rows > 0)), 0.0, -1e30)


def wide_tables(cos, sin):
    return jnp.concatenate([cos, cos], axis=1), jnp.concatenate([-sin, sin], axis=1)


def row_tables(cos_ref, sin_ref, row_start):
    at = pl.ds(pl.multiple_of(row_start, ROWS), ROWS)
    return wide_tables(cos_ref[at, :], sin_ref[at, :])


def head_queries(query, row_cos, row_sin, head):
    start = head * HEAD
    plain = query[:, start : start + NOPE].astype(BF)
    return plain, turn(query[:, start + NOPE : start + HEAD], row_cos, row_sin).astype(BF)


def attention_kernel(
    place_ref,
    mine_ref,
    other_ref,
    query_ref,
    gain_ref,
    kv_up_ref,
    out_weight_ref,
    cos_ref,
    sin_ref,
    seg_keys_ref,
    seg_rows_ref,
    give_ref,
    keep_ref,
    attended_ref,
    compressed_ref,
    kv_ref,
    key_rot_ref,
    log_total_ref,
    peak_ref,
    latent,
    attended,
):
    core = place_ref[1]
    half = ROWS // 2
    for block in range(SPAN):
        start = pl.multiple_of(block * ROWS + core * half, half)
        latent[pl.ds(start, half), :] = mine_ref[block]
        start = pl.multiple_of(block * ROWS + (1 - core) * half, half)
        latent[pl.ds(start, half), :] = other_ref[block]
    inputs = latent[:, :KVRANK].astype(F32)
    inverse = lax.rsqrt(jnp.mean(inputs * inputs, axis=1, keepdims=True) + EPSILON)
    compressed_ref[...] = (inputs * inverse * gain_ref[...]).astype(BF)
    kv_ref[...] = dot(compressed_ref[...], kv_up_ref[...]).astype(BF)
    cosine, sine = wide_tables(cos_ref[...], sin_ref[...])
    key_rot_ref[...] = turn(latent[:, KVRANK:].astype(F32), cosine, sine).astype(BF)
    seg_rows = seg_rows_ref[:, pl.ds(pl.multiple_of(place_ref[3], ROWS), ROWS)]
    bias = mask_bias(seg_keys_ref[...], seg_rows, place_ref[3])
    row_cos, row_sin = row_tables(cos_ref, sin_ref, place_ref[3])
    for head in range(HEADS):
        plain, turned = head_queries(query_ref, row_cos, row_sin, head)
        start = head * (NOPE + VDIM)
        scores = dot(kv_ref[:, start : start + NOPE], plain, NT)
        scores = (scores + dot(key_rot_ref[...], turned, NT)) * SCALE + bias
        peak = jnp.max(scores, axis=0, keepdims=True)
        powers = jnp.exp(scores - peak)
        total = jnp.sum(powers, axis=0, keepdims=True)
        log_total_ref[head : head + 1, :] = peak + jnp.log(total)
        peak_ref[head : head + 1, :] = peak
        weights = (powers * (1.0 / total)).astype(BF)
        values = kv_ref[:, start + NOPE : start + NOPE + VDIM]
        attended[:, head * VDIM : (head + 1) * VDIM] = dot(values, weights, TN).T
    attended_ref[...] = attended[...].astype(BF)
    for block in range(RING):
        for out, which in ((give_ref, 1 - core), (keep_ref, core)):
            start = pl.multiple_of(block * 2 * OWN + which * OWN, OWN)
            out[block] = dot(
                attended[pl.ds(start, OWN), :].astype(BF), out_weight_ref[...]
            ).astype(out.dtype)


def attention(place, mine, other, query, gain, kv_up, out_weight, tables, segs):
    shape = jax.ShapeDtypeStruct
    args = (mine, other, query, gain.reshape(1, KVRANK), kv_up, out_weight, *tables, *segs)
    outs = [
        shape((RING, OWN, D), BF),
        shape((RING, OWN, D), F32),
        shape((ROWS, HEADS * VDIM), BF),
        shape((GROUP, KVRANK), BF),
        shape((GROUP, HEADS * (NOPE + VDIM)), BF),
        shape((GROUP, ROPE), BF),
        shape((HEADS, ROWS), F32),
        shape((HEADS, ROWS), F32),
    ]
    return pl.pallas_call(
        attention_kernel,
        grid_spec=pltpu.PrefetchScalarGridSpec(
            num_scalar_prefetch=1,
            grid=(1,),
            in_specs=[whole(*arg.shape) for arg in args],
            out_specs=[whole(*out.shape) for out in outs],
            scratch_shapes=[
                pltpu.VMEM((GROUP, LATENT), BF),
                pltpu.VMEM((ROWS, HEADS * VDIM), F32),
            ],
        ),
        out_shape=outs,
        compiler_params=pltpu.CompilerParams(vmem_limit_bytes=VMEM_LIMIT),
        cost_estimate=cost(3e9, 14 << 20, 2 * GROUP * ROWS),
        name="attention_forward",
    )(place, *args)


def attention_back_kernel(
    place_ref,
    mine_ref,
    other_ref,
    query_ref,
    compressed_ref,
    kv_ref,
    key_rot_ref,
    log_total_ref,
    kv_up_ref,
    out_weight_ref,
    cos_ref,
    sin_ref,
    seg_keys_ref,
    seg_rows_ref,
    q_weight_ref,
    give_ref,
    keep_ref,
    kv_grad_ref,
    query_grad_ref,
    branch_ref,
    normed_give_ref,
    normed_keep_ref,
    comp_grad,
    rot_grad,
):
    core = place_ref[1]
    interleave(core, mine_ref, other_ref, branch_ref, D + EXTRA)
    attended_grad = dot(branch_ref[:, :D], out_weight_ref[...], NT).astype(BF)
    seg_rows = seg_rows_ref[:, pl.ds(pl.multiple_of(place_ref[3], ROWS), ROWS)]
    bias = mask_bias(seg_keys_ref[...], seg_rows, place_ref[3])
    row_cos, row_sin = row_tables(cos_ref, sin_ref, place_ref[3])
    turned_sum = 0.0
    query_grads = []
    for head in range(HEADS):
        plain, turned = head_queries(query_ref, row_cos, row_sin, head)
        start = head * (NOPE + VDIM)
        keys = kv_ref[:, start : start + NOPE]
        values = kv_ref[:, start + NOPE : start + NOPE + VDIM]
        key_rot = key_rot_ref[...]
        scores = (dot(keys, plain, NT) + dot(key_rot, turned, NT)) * SCALE + bias
        probs = jnp.exp(scores - log_total_ref[head : head + 1, :])
        grad = attended_grad[:, head * VDIM : (head + 1) * VDIM]
        value_grad = dot(probs.astype(BF), grad)
        prob_grad = dot(values, grad, NT)
        inner = jnp.sum(probs * prob_grad, axis=0, keepdims=True)
        score_grad = (probs * (prob_grad - inner)).astype(BF)
        kv_grad_ref[:, start : start + NOPE] = (dot(score_grad, plain) * SCALE).astype(BF)
        kv_grad_ref[:, start + NOPE : start + NOPE + VDIM] = value_grad.astype(BF)
        turned_sum = turned_sum + dot(score_grad, turned) * SCALE
        query_grads.append((dot(keys, score_grad, TN) * SCALE).T)
        turned_grad = (dot(key_rot, score_grad, TN) * SCALE).T
        query_grads.append(turn(turned_grad, row_cos, -row_sin))
    comp_grad[...] = dot(kv_grad_ref[...], kv_up_ref[...], NT)
    cosine, sine = wide_tables(cos_ref[...], sin_ref[...])
    rot_grad[...] = turn(turned_sum, cosine, -sine)
    for block in range(SPAN):
        for inner in range(RING):
            for out, which in ((give_ref, 1 - core), (keep_ref, core)):
                start = pl.multiple_of(block * ROWS + inner * 2 * OWN + which * OWN, OWN)
                out[block, inner, :, :KVRANK] = comp_grad[pl.ds(start, OWN), :].astype(out.dtype)
                out[block, inner, :, KVRANK:] = rot_grad[pl.ds(start, OWN), :].astype(out.dtype)
    query_grad_ref[...] = jnp.concatenate(query_grads, axis=1).astype(BF)
    for block in range(RING):
        for out, which in ((normed_give_ref, 1 - core), (normed_keep_ref, core)):
            start = pl.multiple_of(block * 2 * OWN + which * OWN, OWN)
            part = query_grad_ref[pl.ds(start, OWN), :]
            out[block] = dot(part, q_weight_ref[...], NT).astype(out.dtype)


def attention_back(
    place, mine, other, query, compressed, kv, key_rot, log_total, kv_up, out_weight, tables, segs,
    q_weight,
):
    shape = jax.ShapeDtypeStruct
    args = (
        mine, other, query, compressed, kv, key_rot, log_total, kv_up, out_weight, *tables, *segs,
        q_weight,
    )
    outs = [
        shape((SPAN, RING, OWN, LATENT), BF),
        shape((SPAN, RING, OWN, LATENT), F32),
        shape((GROUP, HEADS * (NOPE + VDIM)), BF),
        shape((ROWS, HEADS * HEAD), BF),
        shape((ROWS, D + EXTRA), BF),
        shape((RING, OWN, D), BF),
        shape((RING, OWN, D), F32),
    ]
    return pl.pallas_call(
        attention_back_kernel,
        grid_spec=pltpu.PrefetchScalarGridSpec(
            num_scalar_prefetch=1,
            grid=(1,),
            in_specs=[whole(*arg.shape) for arg in args],
            out_specs=[whole(*out.shape) for out in outs],
            scratch_shapes=[pltpu.VMEM((GROUP, KVRANK), F32), pltpu.VMEM((GROUP, ROPE), F32)],
        ),
        out_shape=outs,
        compiler_params=pltpu.CompilerParams(vmem_limit_bytes=VMEM_LIMIT),
        cost_estimate=cost(4e9, 16 << 20, 2 * GROUP * ROWS),
        name="attention_backward",
    )(place, *args)


UP_ROWS = KVRANK // 16
BIG = HEADS * HEAD + ATT + 128


def projection_grad_kernel(
    normed, branch, compressed, query_grad, attended, kv_grad, out
):
    width = HEADS * HEAD
    out[:, :width] = dot(normed[...], query_grad[...], TN).astype(BF)
    out[:, width : width + ATT] = dot(branch[...], attended[...], TN).astype(BF)
    up = dot(compressed[...], kv_grad[...], TN)
    for index in range(4):
        for part in range(4):
            start = index * 128 + part * UP_ROWS
            out[start : start + UP_ROWS, width + ATT :] = up[
                index * UP_ROWS : (index + 1) * UP_ROWS, part * 128 : (part + 1) * 128
            ].astype(BF)


def projection_grads(normed, branch, compressed, query_grad, attended, kv_grad):
    block = 512
    return pl.pallas_call(
        projection_grad_kernel,
        grid=(D // block,),
        in_specs=[
            pl.BlockSpec((ROWS, block), lambda i: (0, i)),
            pl.BlockSpec((ROWS, block), lambda i: (0, i)),
            pl.BlockSpec((GROUP, 128), lambda i: (0, i)),
            whole(ROWS, HEADS * HEAD),
            whole(ROWS, ATT),
            whole(GROUP, HEADS * (NOPE + VDIM)),
        ],
        out_specs=pl.BlockSpec((block, BIG), lambda i: (i, 0)),
        out_shape=jax.ShapeDtypeStruct((D, BIG), BF),
        compiler_params=pltpu.CompilerParams(vmem_limit_bytes=VMEM_LIMIT),
        cost_estimate=cost(2e9, 10 << 20),
        name="projection_grads",
    )(normed, branch, compressed, query_grad, attended, kv_grad)


def combine_kernel(place_ref, pick_ref, returned_ref, shared_ref, give_ref, keep_ref, total):
    core = place_ref[1]
    rows = dot(pick_ref[...], returned_ref[...], TN)
    total[:, :D] = shared_ref[...]
    mine = pl.ds(pl.multiple_of(core * HALF, HALF), HALF)
    total[:, mine] = total[:, mine] + rows[:, :HALF]
    if returned_ref.shape[1] > HALF:
        total[:, D:] = rows[:, HALF:]
    for block in range(RING):
        for out, which in ((give_ref, 1 - core), (keep_ref, core)):
            start = pl.multiple_of(block * 2 * OWN + which * OWN, OWN)
            out[block] = total[pl.ds(start, OWN), :].astype(out.dtype)


def combine_rows(place, pick, returned, shared):
    width = D + returned.shape[1] - HALF
    args = (pick, returned, shared)
    outs = [
        jax.ShapeDtypeStruct((RING, OWN, width), BF),
        jax.ShapeDtypeStruct((RING, OWN, width), F32),
    ]
    return pl.pallas_call(
        combine_kernel,
        grid_spec=pltpu.PrefetchScalarGridSpec(
            num_scalar_prefetch=1,
            grid=(1,),
            in_specs=[whole(*arg.shape) for arg in args],
            out_specs=[whole(*out.shape) for out in outs],
            scratch_shapes=[pltpu.VMEM((ROWS, width), F32)],
        ),
        out_shape=outs,
        compiler_params=pltpu.CompilerParams(vmem_limit_bytes=VMEM_LIMIT),
        cost_estimate=cost(7e8, 8 << 20),
        name="combine_rows",
    )(place, *args)


def order_kernel(x_ref, *refs):
    for step in range(RING):
        refs[RING][lax.rem(x_ref[0] + RING - step, RING)] = refs[step][...]


def order_ring(x, blocks):
    rows, width = blocks[0].shape
    return pl.pallas_call(
        order_kernel,
        grid_spec=pltpu.PrefetchScalarGridSpec(
            num_scalar_prefetch=1,
            grid=(1,),
            in_specs=[whole(rows, width)] * RING,
            out_specs=whole(RING, rows, width),
        ),
        out_shape=jax.ShapeDtypeStruct((RING, rows, width), blocks[0].dtype),
        cost_estimate=cost(0, 2 << 20),
        name="order_ring",
    )(x.reshape(1), *blocks)


def interleave(core, mine_ref, other_ref, out, width):
    for block in range(RING):
        for ref, which in ((mine_ref, core), (other_ref, 1 - core)):
            start = pl.multiple_of(block * 2 * OWN + which * OWN, OWN)
            out[pl.ds(start, OWN), :] = ref[block, :, :width]


def gating_kernel(
    place_ref, mine_ref, other_ref, router_ref, pick_ref, grad_ref, mixed_ref, probs_ref, sent_ref
):
    core = place_ref[1]
    interleave(core, mine_ref, other_ref, mixed_ref, D)
    logits = dot(mixed_ref[...], router_ref[...])
    powers = jnp.exp(logits - jnp.max(logits, axis=1, keepdims=True))
    probs = powers / jnp.sum(powers, axis=1, keepdims=True)
    probs_ref[...] = probs
    pick = pick_ref[...]
    high = probs.astype(BF)
    rest = probs - high.astype(F32)
    middle = rest.astype(BF)
    low = (rest - middle.astype(F32)).astype(BF)
    gates = dot(pick, high) + dot(pick, middle) + dot(pick, low)
    slot = lax.broadcasted_iota(jnp.int32, (SLOTS, EXPERTS), 0)
    lane = lax.broadcasted_iota(jnp.int32, (SLOTS, EXPERTS), 1)
    first = (lane - place_ref[0]) * (CAP // 4)
    inside = (slot >= first) & (slot < first + CAP) & (lax.rem(lane, 4) == place_ref[0])
    gate = jnp.sum(jnp.where(inside, gates, 0.0), axis=1, keepdims=True)
    high = gate.astype(BF).astype(F32)
    lane = lax.broadcasted_iota(jnp.int32, (SLOTS, EXTRA), 1)
    sent_ref[:, D:] = jnp.where(
        lane == 0, high, jnp.where(lane == 1, gate - high, 0.0)
    ).astype(BF)
    mine = pl.ds(pl.multiple_of(core * HALF, HALF), HALF)
    sent_ref[:, :HALF] = dot(pick, mixed_ref[:, mine]).astype(BF)
    sent_ref[:, HALF:D] = dot(pick, grad_ref[:, mine]).astype(BF)


def gating(place, mine, other, router, pick, out_grad):
    args = (mine, other, router, pick, out_grad)
    outs = [
        jax.ShapeDtypeStruct((ROWS, D), BF),
        jax.ShapeDtypeStruct((ROWS, EXPERTS), F32),
        jax.ShapeDtypeStruct((SLOTS, D + EXTRA), BF),
    ]
    return pl.pallas_call(
        gating_kernel,
        grid_spec=pltpu.PrefetchScalarGridSpec(
            num_scalar_prefetch=1,
            grid=(1,),
            in_specs=[whole(*arg.shape) for arg in args],
            out_specs=[whole(*out.shape) for out in outs],
        ),
        out_shape=outs,
        compiler_params=pltpu.CompilerParams(vmem_limit_bytes=VMEM_LIMIT),
        cost_estimate=cost(8e8, 6 << 20),
        name="gating",
    )(place, *args)


KD_COLUMNS = LATENT // 8
ROUTER_COLUMNS = EXPERTS // 8
SHARE = KD_COLUMNS + ROUTER_COLUMNS
SMALL = SHARE + 16


def small_kernel(latent, logit, normed, mixed, norm_gain, mix_gain, kv_gain, peak_ref, out):
    kv_down = dot(latent[...], normed[...], TN)
    router = dot(logit[...], mixed[...], TN)
    lane = lax.broadcasted_iota(jnp.int32, (1, 128), 1)
    peak = 0.0
    for head in range(HEADS):
        highest = jnp.max(peak_ref[head : head + 1, :], axis=1, keepdims=True)
        peak = jnp.where(lane == head, highest, peak)

    def parts(row, number):
        found = []
        for _ in range(number):
            found.append(row.astype(BF).astype(F32))
            row = row - found[-1]
        return found

    peaks = parts(peak, 3)
    zeros = jnp.zeros((7, 128), F32)
    for index in range(16):
        at = slice(index * 128, (index + 1) * 128)
        gain = kv_gain[:, index * UP_ROWS : (index + 1) * UP_ROWS]
        gain = jnp.concatenate([gain, jnp.zeros((1, 128 - UP_ROWS), F32)], axis=1)
        rows = parts(norm_gain[:, at], 2) + parts(mix_gain[:, at], 2) + parts(gain, 2)
        rows = [kv_down[:, at], router[:, at]] + rows + peaks + [zeros]
        out[index] = jnp.concatenate(rows, axis=0).astype(BF)


def small_grads(latent, logit, normed, mixed, norm_gain, mix_gain, kv_gain, peak):
    args = (
        latent,
        logit,
        normed,
        mixed,
        norm_gain.reshape(1, D),
        mix_gain.reshape(1, D),
        kv_gain.reshape(1, KVRANK),
        peak,
    )
    return pl.pallas_call(
        small_kernel,
        grid=(1,),
        in_specs=[whole(*arg.shape) for arg in args],
        out_specs=whole(16, SMALL, 128),
        out_shape=jax.ShapeDtypeStruct((16, SMALL, 128), BF),
        compiler_params=pltpu.CompilerParams(vmem_limit_bytes=VMEM_LIMIT),
        cost_estimate=cost(2e8, 4 << 20),
        name="small_grads",
    )(*args)


def split_two(value):
    high = lax.reduce_precision(value, 8, 7)
    return high.astype(BF), (value - high).astype(BF)


def norm_rows(inputs, gain_vec):
    inverse = lax.rsqrt(jnp.mean(inputs * inputs, axis=-1, keepdims=True) + EPSILON)
    return (inputs * inverse * gain_vec, inverse)


def norm_back(inputs, inverse, gain_vec, gradient):
    weighted = gradient * gain_vec
    inner = jnp.mean(weighted * inputs, axis=-1, keepdims=True)
    d_inputs = inverse * weighted - inputs * (inverse * inverse * inverse) * inner
    return (d_inputs, jnp.sum(gradient * inputs * inverse, axis=0))


def rotate(inputs, cosine, sine):
    half_size = inputs.shape[-1] // 2
    first_half = inputs[..., :half_size]
    second_half = inputs[..., half_size:]
    return jnp.concatenate(
        [first_half * cosine - second_half * sine, second_half * cosine + first_half * sine],
        axis=-1,
    )


def unrotate(gradient, cosine, sine):
    return rotate(gradient, cosine, -sine)


def shards(
    tokens,
    out_grad,
    routes,
    segment,
    norm_gain,
    q_weight,
    kv_down,
    kv_gain,
    kv_up,
    out_weight,
    mix_gain,
    router,
    shared_gate,
    shared_up,
    shared_down,
    expert_gate,
    expert_up,
    expert_down,
    step_size,
    threshold,
):
    rows = tokens.shape[0]
    x = lax.axis_index("x")
    c = lax.axis_index("c")
    y = lax.axis_index("y")
    z = lax.axis_index("z")
    j = z * RING + y
    t = x * 2 + c
    heads = q_weight.shape[1] // (NOPE + ROPE)
    group_len = rows * SPAN
    count = expert_down.shape[0] * 4
    score_scale = 1.0 / math.sqrt(NOPE + ROPE)
    own_start = t * OWN

    def own_rows(array):
        return lax.dynamic_slice_in_dim(array, own_start, OWN, 0)

    routes_t = routes.T
    chosen = 4 * jnp.arange(count, dtype=jnp.int32) + x
    hot = jnp.any(routes_t[None, :, :] == chosen[:, None, None], axis=1)
    number = jnp.arange(rows, dtype=jnp.int32)
    earlier = (number[:, None] < number[None, :]).astype(BF)
    slot = dot(hot.astype(BF), earlier)
    pick = hot[:, None, :] & (slot[:, None, :] == jnp.arange(CAP, dtype=F32)[None, :, None])
    pick_b = pick.astype(BF).reshape(count * CAP, rows)

    place = jnp.stack([x, c, 4 * j + x, y * rows]).astype(jnp.int32)

    def send_rows(sent):
        width = sent.shape[1]
        return spread(sent.reshape(count, CAP, width)).reshape(count * CAP, width)

    gate_t = jnp.swapaxes(expert_gate, 1, 2)
    up_t = jnp.swapaxes(expert_up, 1, 2)
    first_part, last_part = pack(x, gate_t, up_t, expert_down)
    first_part = [shift(first_part[step - 1], "x", step) for step in (1, 2, 3)]

    group_ids = lax.dynamic_slice_in_dim(segment, z * group_len, group_len)
    key_number = jnp.arange(group_len, dtype=jnp.int32)
    first_length = jnp.sum((group_ids == 1).astype(jnp.int32))
    key_place = jnp.where(
        group_ids == 0,
        key_number - (group_len - PROMPT),
        key_number + PROMPT - jnp.where(group_ids == 1, 0, first_length),
    )
    frequency = jnp.power(10000.0, -2.0 * jnp.arange(ROPE // 2, dtype=F32) / ROPE)
    key_angle = key_place.astype(F32)[:, None] * frequency[None, :]
    tables = (jnp.cos(key_angle), jnp.sin(key_angle))
    segs = (group_ids.reshape(group_len, 1), group_ids.reshape(1, group_len))

    x_input = after(tokens, last_part[0]).astype(F32)
    normed_f, _ = norm_rows(x_input, norm_gain)
    normed = normed_f.astype(BF)
    latent = dot(normed, kv_down).astype(BF)
    half_latent = lax.dynamic_slice_in_dim(latent, c * (rows // 2), rows // 2, 0)
    gathered = gather_ring(half_latent, "y", y)
    query_lin = dot(normed, q_weight)
    attn_give, attn_keep, attended_b, compressed, kv_rows, key_rot, log_total, row_peak = attention(
        place, gathered, swap(gathered), query_lin, kv_gain, kv_up, out_weight, tables, segs
    )

    attn_got = swap(after(attn_give, *first_part))
    attn_own, attn_sent = ring_parts(attn_keep + attn_got.astype(F32), x)
    residual = own_rows(tokens).astype(F32) + sum_sent(attn_own, attn_sent, "x")
    mixed_f, inverse_two = norm_rows(residual, mix_gain)
    mixed_own = mixed_f.astype(BF)
    mixed_ring = [mixed_own] + [shift(mixed_own, "x", step) for step in (1, 2, 3)]
    mixed_mine = order_ring(x, mixed_ring)
    last_part = [after(piece, mixed_mine) for piece in last_part]
    last_part = [shift(last_part[step - 1], "x", step) for step in (1, 2, 3)]
    packed = (first_part, last_part)
    mixed_other = swap(mixed_mine)

    mixed_in, gate_probs, mixed_sent = gating(
        place, mixed_mine, mixed_other, router, pick_b, out_grad
    )
    mixed_rows = send_rows(mixed_sent)
    shared_part, shared_mixed_grad, shared_grads = shared_experts(
        after(mixed_in, mixed_sent), out_grad, shared_gate.T, shared_up.T, shared_down
    )
    mixed_rows = after(mixed_rows, shared_part, *last_part)
    mixed_rows = (mixed_rows, swap(mixed_rows))
    expert_act, scaled_act, gate_lin_grad, up_lin_grad, grad_keep, grad_give, slot_cols = (
        expert_pass(place, *mixed_rows, gate_t, up_t, expert_down, packed)
    )

    grad_half = (grad_keep + swap(grad_give).astype(F32)).astype(BF)
    sent_grad = jnp.concatenate([grad_half, slot_cols], axis=1)
    returned_grad = send_rows(sent_grad)
    parts = weight_grads(
        place,
        (0, 1, 2),
        (0, 1, 2, 3),
        (gate_lin_grad, up_lin_grad, after(scaled_act, sent_grad)),
        mixed_rows,
    )

    def send_home(part):
        return [part[0]] + [shift(part[step], "x", RING - step) for step in (1, 2, 3)]

    home = [send_home(parts[0])]
    produced_keep, produced_give = produce(
        place, after(expert_act, parts[0][0]), mixed_rows[0], expert_down, packed
    )
    mixed_give, mixed_keep = combine_rows(
        place, pick_b, after(returned_grad, parts[0][0], produced_give), shared_mixed_grad
    )
    mixed_half = mixed_keep + swap(after(mixed_give, *home[0])).astype(F32)
    mixed_half, mixed_sent = ring_parts(mixed_half, x)
    shared_grads = lax.psum_scatter(
        after(shared_grads, mixed_rows[0]), EXPERT, scatter_dimension=0, tiled=True
    )
    produced_half = (produced_keep + swap(produced_give).astype(F32)).astype(BF)
    produced = send_rows(after(produced_half, *mixed_sent))
    mixed_total = sum_sent(mixed_half, mixed_sent, "x")
    prob_grad = mixed_total[:, D : D + EXPERTS] + mixed_total[:, D + EXPERTS :]
    own_probs = own_rows(gate_probs)
    logit_grad = (
        own_probs * (prob_grad - jnp.sum(own_probs * prob_grad, axis=-1, keepdims=True))
    ).astype(BF)
    mixed_grad = mixed_total[:, :D] + dot(logit_grad, router, ((1,), (1,)))
    mid_norm_grad, mix_gain_grad = norm_back(residual, inverse_two, mix_gain, mixed_grad)
    mid_grad = own_rows(out_grad).astype(F32) + mid_norm_grad
    branch_own = jnp.concatenate(
        [mid_grad.astype(BF), logit_grad, jnp.zeros((OWN, 128 - EXPERTS), BF)], axis=1
    )
    branch_ring = [branch_own] + [shift(branch_own, "x", step) for step in (1, 2, 3)]
    branch_mine = order_ring(x, branch_ring)
    home.append(send_home([after(piece, branch_mine) for piece in parts[1]]))
    (
        latent_give, latent_keep, kv_grad, query_lin_grad, branch_all, normed_give, normed_keep,
    ) = attention_back(
        place, branch_mine, swap(branch_mine), query_lin, compressed, kv_rows, key_rot, log_total, kv_up, out_weight,
        tables, segs, q_weight,
    )
    latent_give = after(latent_give, produced, *home[1])
    latent_sent = (latent_keep + swap(latent_give).astype(F32)).astype(BF)
    latent_parts = lax.all_to_all(
        latent_sent.reshape(SPAN * RING, OWN, LATENT), ("y", "x"), split_axis=0, concat_axis=0,
        tiled=True,
    )
    latent_total = jnp.sum(latent_parts.astype(F32), axis=0)
    normed_half = normed_keep + swap(after(normed_give, latent_sent)).astype(F32)
    normed_own, normed_sent = ring_parts(normed_half, x)
    normed_total = sum_sent(normed_own, normed_sent, "x")

    logit_grad_all = branch_all[:, D : D + EXPERTS]
    own_comp = own_rows(latent)[:, :KVRANK].astype(F32)
    _, own_inverse = norm_rows(own_comp, kv_gain)
    comp_own_grad, kv_gain_grad = norm_back(
        own_comp, own_inverse, kv_gain, latent_total[:, :KVRANK]
    )
    latent_grad = jnp.concatenate([comp_own_grad, latent_total[:, KVRANK:]], axis=-1).astype(BF)
    latent_columns = jnp.swapaxes(latent_grad.reshape(OWN, 8, KD_COLUMNS), 0, 1)
    big = projection_grads(
        normed, branch_all, compressed, query_lin_grad, attended_b, after(kv_grad, latent_columns)
    )
    latent_columns = lax.all_to_all(
        latent_columns, TENSOR, split_axis=0, concat_axis=0, tiled=True
    )
    normed_grad = normed_total + dot(latent_grad, kv_down, ((1,), (1,)))
    own_input = own_rows(tokens).astype(F32)
    _, inverse_one = norm_rows(own_input, norm_gain)
    input_norm_grad, norm_gain_grad = norm_back(own_input, inverse_one, norm_gain, normed_grad)


    up_rows = UP_ROWS
    kd_width = KD_COLUMNS
    rt_width = ROUTER_COLUMNS
    small = small_grads(
        latent_columns.reshape(rows, kd_width),
        lax.dynamic_slice_in_dim(logit_grad_all, t * rt_width, rt_width, 1),
        normed,
        mixed_in,
        norm_gain_grad,
        mix_gain_grad,
        kv_gain_grad,
        row_peak,
    )
    small = jnp.swapaxes(small.reshape(count, 6, 16, 128), 1, 2).reshape(count, 16, BIG)
    packed_grads = jnp.concatenate([big.reshape(count, 128, BIG), small], axis=1)
    home.append(send_home([after(piece, *normed_sent) for piece in parts[2]]))
    packed_grads = after(packed_grads, *home[2])
    packed_sent = packed_grads
    packed_grads = spread(packed_grads)
    small = jnp.swapaxes(packed_grads[:, 128:].reshape(count, 16, 6, 128), 1, 2)
    small = small.reshape(count, SMALL, 128)
    layer_give, layer_keep = combine_rows(
        place, pick_b, after(produced, packed_sent), shared_part
    )
    layer_half = layer_keep + swap(layer_give).astype(F32)
    home.append(send_home([after(piece, packed_sent) for piece in parts[3]]))
    layer_total = residual + sum_ring(after(layer_half, *home[3]), "x", x)
    layer_out = gather_rows(layer_total.astype(BF))
    tokens_grad = gather_rows((mid_grad + input_norm_grad).astype(BF)).astype(F32)
    shared_sum = after(shared_grads, layer_total).astype(F32)
    shared_gate_grad = shared_sum[:, :SHARED]
    shared_up_grad = shared_sum[:, WIDE : WIDE + SHARED]
    shared_down_grad = shared_sum[:, 2 * WIDE : 2 * WIDE + SHARED].T
    big = jnp.sum(packed_grads[:, :128].astype(F32), axis=0)
    q_width = q_weight.shape[1]
    q_weight_grad = big[:, :q_width]
    out_weight_grad = big[:, q_width : q_width + ATT].T
    kv_up_grad = jnp.swapaxes(big[:, q_width + ATT :].reshape(4, up_rows, 128), 0, 1).reshape(
        up_rows, 4 * 128
    )

    small = small.astype(F32)
    wide = kd_width + rt_width
    small_sum = jnp.sum(small[:, : wide + 6], axis=0)
    peaks = small[:, wide + 6 : wide + 9, :heads]
    top_peak = jnp.max(peaks[:, 0] + peaks[:, 1] + peaks[:, 2], axis=0)
    vectors = small_sum[wide : wide + 6].reshape(3, 2, 128).sum(axis=1)
    vector_high, vector_low = split_two(vectors)
    shared_small = jnp.concatenate(
        [small_sum[:wide].astype(BF), vector_high, vector_low, jnp.zeros((10, 128), BF)], axis=0
    )
    all_small = lax.all_to_all(
        jnp.broadcast_to(shared_small[None], (8, wide + 16, 128)), TENSOR, split_axis=0,
        concat_axis=0, tiled=True,
    )
    expert_gate_grad, expert_up_grad, expert_down_grad = unpack(
        x, [after(home[0], shared_small), *home[1:]]
    )
    all_small = after(all_small, expert_gate_grad, tokens_grad)
    expert_gate_grad = jnp.swapaxes(expert_gate_grad, 1, 2)
    expert_up_grad = jnp.swapaxes(expert_up_grad, 1, 2)
    kv_down_grad = all_small[:, :kd_width].reshape(8 * kd_width, 128).T.astype(F32)
    router_grad = all_small[:, kd_width:wide].reshape(8 * rt_width, 128).T.astype(F32)
    vectors = jnp.sum(all_small[:, wide : wide + 6].astype(F32), axis=0).reshape(2, 3, 128).sum(axis=0)
    norm_gain_grad = vectors[0]
    mix_gain_grad = vectors[1]
    kv_gain_grad = vectors[2, : KVRANK // count]

    factor = jnp.minimum(1.0, threshold[0] / jnp.maximum(top_peak, 1.0))
    root_factor = jnp.sqrt(factor)
    q_rows = q_weight.shape[0] // count
    own_query = lax.dynamic_slice_in_dim(q_weight, j * q_rows, q_rows, 0).astype(F32)
    query_step = (own_query - step_size[0] * q_weight_grad).reshape(q_rows, heads, NOPE + ROPE)
    q_weight_new = jnp.concatenate(
        [
            query_step[..., :NOPE] * root_factor[None, :, None],
            query_step[..., NOPE:] * factor[None, :, None],
        ],
        axis=-1,
    ).reshape(q_rows, heads * (NOPE + ROPE))
    own_up = lax.dynamic_slice_in_dim(kv_up, j * up_rows, up_rows, 0).astype(F32)
    up_step = (own_up - step_size[0] * kv_up_grad).reshape(up_rows, heads, NOPE + VDIM)
    kv_up_new = jnp.concatenate(
        [up_step[..., :NOPE] * root_factor[None, :, None], up_step[..., NOPE:]], axis=-1
    ).reshape(up_rows, heads * (NOPE + VDIM))
    return (
        layer_out,
        tokens_grad,
        q_weight_grad,
        kv_down_grad,
        kv_up_grad,
        out_weight_grad,
        router_grad,
        norm_gain_grad,
        kv_gain_grad,
        mix_gain_grad,
        shared_gate_grad,
        shared_up_grad,
        shared_down_grad,
        expert_gate_grad,
        expert_up_grad,
        expert_down_grad,
        q_weight_new,
        kv_up_new,
    )


def solution(mesh):
    fine = Mesh(mesh.devices.reshape(4, 4, 4, 2), ("z", "y", "x", "c"))
    return jax.shard_map(
        shards,
        mesh=fine,
        in_specs=(
            P(EXPERT, None),
            P(EXPERT, None),
            P(EXPERT, None),
            P(),
            P(),
            P(None, TENSOR),
            P(),
            P(),
            P(None, TENSOR),
            P(TENSOR, None),
            P(),
            P(),
            P(None, TENSOR),
            P(None, TENSOR),
            P(TENSOR, None),
            P(EXPERT, None, TENSOR),
            P(EXPERT, None, TENSOR),
            P(EXPERT, TENSOR, None),
            P(),
            P(),
        ),
        out_specs=(
            P(EXPERT, None),
            P(EXPERT, None),
            P(EXPERT, TENSOR),
            P(EXPERT, None),
            P(EXPERT, TENSOR),
            P(TENSOR, EXPERT),
            P(EXPERT, None),
            P(EXPERT),
            P(EXPERT),
            P(EXPERT),
            P(EXPERT, TENSOR),
            P(EXPERT, TENSOR),
            P(TENSOR, EXPERT),
            P(EXPERT, None, TENSOR),
            P(EXPERT, None, TENSOR),
            P(EXPERT, TENSOR, None),
            P(EXPERT, TENSOR),
            P(EXPERT, TENSOR),
        ),
        check_vma=False,
    )
```

profile of v0, /device:TPU:1, one launch (start us, length us, event | category | flops | bytes accessed | tf_op | source)
XLA Modules:
  0.0 526.0 jit_solution(12926920326525339042)
XLA Ops:
  8.1 6.4 %pack_weights.1 = (bf16[208,2048]{1,0:T(8,128)(2,1)}, bf16[320,2048]{1,0:T(8,128)(2,1)}, bf16[208,2048]{1,0:T(8,128)(2,1)}, bf16[320,2048]{1,0:T(8,128)(2,1)}, b...) custom-call(s32[1]{0:T(128)} %bitcast.x_ref, bf16[4,176,2048]{2,1,0:T(8,128)(2,1)} %bitcast.149, ...), custom_call_target="tpu_custom_call" | custom-call | bytes 212992 | tf_op jit(solution)/shard_map/pack_weights/pallas_call | solution.py:156
  19.3 3.7 collective-permute-start.1
  47.1 4.3 multiply_sine_fusion
  52.4 11.7 %attention_forward.1 = (bf16[4,48,2048]{2,1,0:T(8,128)(2,1)}, f32[4,48,2048]{2,1,0:T(8,128)}, bf16[384,256]{1,0:T(8,128)(2,1)}, bf16[1536,512]{1,0:T(8,128)(2,1)...) custom-call(s32[4]{0:T(128)} %pad_add_fusion.place_ref, ...), custom_call_target="tpu_custom_call" | custom-call | flops 46875000 | bytes 229376 | tf_op jit(solution)/shard_map/attention_forward/pallas_call | solution.py:545
  81.0 4.8 collective-permute-done.9
  96.1 5.4 %collective-permute-done.11.refs_1_ = bf16[48,2048]{1,0:T(8,128)(2,1)} collective-permute-done((bf16[48,2048]{1,0:T(8,128)(2,1)S(1)}, bf16[48,2048]{1,0:T(8,128)(2,1)}, u32[]{:S(2)}, u32[]{:S(2)}) %collective-permute-start.11) | collective-permute-done | bytes 196640 | tf_op jit(solution)/shard_map/ppermute | solution.py:43
  107.2 8.3 %gating.1 = (bf16[384,2048]{1,0:T(8,128)(2,1)}, f32[384,64]{1,0:T(8,128)}, bf16[768,2176]{1,0:T(8,128)(2,1)}) custom-call(s32[4]{0:T(128)} %pad_add_fusion.place_ref, bf16[4,48,2048]{2,1,0:T(8,128)(2,1)} %order_ring.2.mine_ref, bf16[4,48,2048]{2,1,0:T(8,128)(2,1)} %collective-permute-done.14.other_ref, bf16[2048,64]{1,0:T(8,128)(2,1)} %copy.79.router_ref, ...), custom_call_target="tpu_custom_call" | custom-call | flops 12500000 | bytes 98304 | tf_op jit(solution)/shard_map/gating/pallas_call | solution.py:810
  115.5 5.2 all-to-all-start
  123.4 14.3 %shared_experts.1 = (f32[384,2048]{1,0:T(8,128)}, f32[384,2048]{1,0:T(8,128)}, bf16[2048,1152]{1,0:T(8,128)(2,1)}) custom-call(bf16[384,2048]{1,0:T(8,128)(2,1)} %get-tuple-element.124.mixed, bf16[384,2048]{1,0:T(8,128)(2,1)} %out_grad.1, bf16[352,2048]{1,0:T(8,128)(2,1)} %bitcast.168, bf16[352,2048]{1,0:T(8,128)(2,1)} %bitcast.169, bf16[352,2048]{1,0:T(8,128)(2,1)} %down_w.1), custom_call_target="tpu_custom_call" | custom-call | flops 77856768 | bytes 294912 | tf_op jit(solution)/shard_map/shared_experts/pallas_call | solution.py:424
  137.7 42.5 %collective-permute-done.15.q1.p1 = bf16[320,2048]{1,0:T(8,128)(2,1)} collective-permute-done((bf16[320,2048]{1,0:T(8,128)(2,1)}, bf16[320,2048]{1,0:T(8,128)(2,1)}, u32[]{:S(2)}, u32[]{:S(2)}) %collective-permute-start.15) | collective-permute-done | bytes 1310752 | tf_op jit(solution)/shard_map/ppermute | solution.py:43
  182.6 5.8 %collective-permute-done.18.other_ref.grad_other_ref.refs_4_.refs_6_ = bf16[768,2176]{1,0:T(8,128)(2,1)S(1)} collective-permute-done((bf16[768,2176]{1,0:T(8,128)(2,1)}, bf16[768,2176]{1,0:T(8,128)(2,1)S(1)}, u32[]{:S(2)}, u32[]{:S(2)}) %collective-permute-start.18) | collective-permute-done | bytes 3342368 | tf_op jit(solution)/shard_map/ppermute | solution.py:39
  190.1 20.5 %expert_pass.1 = (bf16[768,704]{1,0:T(8,128)(2,1)}, bf16[768,704]{1,0:T(8,128)(2,1)}, bf16[768,704]{1,0:T(8,128)(2,1)}, bf16[768,704]{1,0:T(8,128)(2,1)}, f32[76...) custom-call(s32[4]{0:T(128)} %pad_add_fusion.place_ref, ...), custom_call_target="tpu_custom_call" | custom-call | flops 173015040 | bytes 393216 | tf_op jit(solution)/shard_map/expert_pass/pallas_call | solution.py:292
  218.3 6.6 %all-to-all-start.1 = ((bf16[16,48,1152]{2,1,0:T(8,128)(2,1)}), bf16[16,48,1152]{2,1,0:T(8,128)(2,1)}, u32[]{:S(2)}, u32[]{:S(2)}) async-start(bf16[16,48,1152]{2,1,0:T(8,128)(2,1)} %bitcast.158), calls=%async_computation.1 | async-start | bytes 3538944 | tf_op jit(solution)/shard_map/all_to_all | solution.py:47
  225.0 13.5 %weight_grads.1 = (bf16[96,2048]{1,0:T(8,128)(2,1)}, bf16[96,2048]{1,0:T(8,128)(2,1)}, bf16[96,2048]{1,0:T(8,128)(2,1)}, bf16[96,2048]{1,0:T(8,128)(2,1)}, bf16[...) custom-call(s32[4]{0:T(128)} %pad_add_fusion.place_ref, ...), custom_call_target="tpu_custom_call" | custom-call | flops 103809024 | bytes 294912 | tf_op jit(solution)/shard_map/weight_grads/pallas_call | solution.py:371
  241.3 7.8 %produce.1 = (f32[768,1024]{1,0:T(8,128)}, bf16[768,1024]{1,0:T(8,128)(2,1)}) custom-call(s32[4]{0:T(128)} %pad_add_fusion.place_ref, bf16[768,704]{1,0:T(8,128)(2,1)} %get-tuple-element.141.act_ref, bf16[768,2176]{1,0:T(8,128)(2,1)} %bitcast.19.mine_ref.grad_mine_ref.gate_ref.refs_3_.refs_5_, bf16[4,176,2048]{2,1,0:T(8,128)(2,1)} %own_down.3, ...), custom_call_target="tpu_custom_call" | custom-call | flops 34603008 | bytes 147456 | tf_op jit(solution)/shard_map/produce/pallas_call | solution.py:324
  252.1 5.9 %combine_rows.2 = (bf16[4,48,2176]{2,1,0:T(8,128)(2,1)}, f32[4,48,2176]{2,1,0:T(8,128)}) custom-call(s32[4]{0:T(128)} %pad_add_fusion.place_ref, bf16[768,384]{1,0:T(8,128)(2,1)} %fusion.4.pick_ref, bf16[768,1152]{1,0:T(8,128)(2,1)} %bitcast.23.returned_ref, f32[384,2048]{1,0:T(8,128)} %get-tuple-element.145.shared_ref), custom_call_target="tpu_custom_call" | custom-call | flops 10937500 | bytes 131072 | tf_op jit(solution)/shard_map/combine_rows/pallas_call | solution.py:729
  273.3 6.7 %all-to-all-start.2 = ((bf16[16,48,1024]{2,1,0:T(8,128)(2,1)}), bf16[16,48,1024]{2,1,0:T(8,128)(2,1)}, u32[]{:S(2)}, u32[]{:S(2)}) async-start(bf16[16,48,1024]{2,1,0:T(8,128)(2,1)} %bitcast.159), calls=%async_computation.2 | async-start | bytes 3145728 | tf_op jit(solution)/shard_map/all_to_all | solution.py:47
  290.3 4.4 collective-permute-done.30.refs_3_
  295.4 6.0 %collective-permute-done.28.refs_1_ = bf16[48,2176]{1,0:T(8,128)(2,1)} collective-permute-done((bf16[48,2176]{1,0:T(8,128)(2,1)S(1)}, bf16[48,2176]{1,0:T(8,128)(2,1)}, u32[]{:S(2)}, u32[]{:S(2)}) %collective-permute-start.28) | collective-permute-done | bytes 208928 | tf_op jit(solution)/shard_map/ppermute | solution.py:43
  307.5 18.7 %attention_backward.1 = (bf16[4,4,48,576]{3,2,1,0:T(8,128)(2,1)}, f32[4,4,48,576]{3,2,1,0:T(8,128)}, bf16[1536,512]{1,0:T(8,128)(2,1)}, bf16[384,384]{1,0:T(8,12...) custom-call(s32[4]{0:T(128)} %pad_add_fusion.place_ref, ...), custom_call_target="tpu_custom_call" | custom-call | flops 62500000 | bytes 262144 | tf_op jit(solution)/shard_map/attention_backward/pallas_call | solution.py:652
  339.2 4.5 all-to-all-start.3
  355.5 4.5 all-to-all-done.3
  364.6 5.8 %all-to-all-start.4 = ((bf16[8,48,72]{2,1,0:T(8,128)(2,1)}), bf16[8,48,72]{2,1,0:T(8,128)(2,1)S(1)}, u32[]{:S(2)}, u32[]{:S(2)}) async-start(bf16[8,48,72]{2,1,0:T(8,128)(2,1)} %bitcast.145), calls=%async_computation.4 | async-start | bytes 196608 | tf_op jit(solution)/shard_map/all_to_all | solution.py:1090
  370.4 6.8 %projection_grads.1 = bf16[2048,768]{1,0:T(8,128)(2,1)} custom-call(bf16[384,2048]{1,0:T(8,128)(2,1)} %copy-done.2, bf16[384,2176]{1,0:T(8,128)(2,1)} %get-tuple-element.158.branch, bf16[1536,512]{1,0:T(8,128)(2,1)} %get-tuple-element.154.compressed_ref.compressed, bf16[384,384]{1,0:T(8,128)(2,1)} %get-tuple-element.159.query_grad, ...), custom_call_target="tpu_custom_call" | custom-call | flops 31250000 | bytes 163840 | tf_op jit(solution)/shard_map/projection_grads/pallas_call | solution.py:689
  388.3 4.1 pad_maximum_fusion
  392.9 5.0 all-to-all-start.5
  399.9 5.8 %combine_rows.3 = (bf16[4,48,2048]{2,1,0:T(8,128)(2,1)}, f32[4,48,2048]{2,1,0:T(8,128)}) custom-call(s32[4]{0:T(128)} %pad_add_fusion.place_ref, bf16[768,384]{1,0:T(8,128)(2,1)} %fusion.4.pick_ref, bf16[768,1024]{1,0:T(8,128)(2,1)} %bitcast.28.returned_ref, f32[384,2048]{1,0:T(8,128)} %get-tuple-element.125.shared_ref), custom_call_target="tpu_custom_call" | custom-call | flops 10937500 | bytes 131072 | tf_op jit(solution)/shard_map/combine_rows/pallas_call | solution.py:729
  412.0 24.0 %collective-permute-done.44.refs_13_ = bf16[240,2048]{1,0:T(8,128)(2,1)S(1)} collective-permute-done((bf16[240,2048]{1,0:T(8,128)(2,1)S(1)}, bf16[240,2048]{1,0:T(8,128)(2,1)S(1)}, u32[]{:S(2)}, u32[]{:S(2)}) %collective-permute-start.44) | collective-permute-done | bytes 983072 | tf_op jit(solution)/shard_map/ppermute | solution.py:43
  437.0 24.2 %collective-permute-done.46.refs_15_ = bf16[240,2048]{1,0:T(8,128)(2,1)S(1)} collective-permute-done((bf16[240,2048]{1,0:T(8,128)(2,1)S(1)}, bf16[240,2048]{1,0:T(8,128)(2,1)S(1)}, u32[]{:S(2)}, u32[]{:S(2)}) %collective-permute-start.46) | collective-permute-done | bytes 983072 | tf_op jit(solution)/shard_map/ppermute | solution.py:43
  465.4 7.3 %collective-permute-done.47 = bf16[48,2048]{1,0:T(8,128)(2,1)S(1)} collective-permute-done((bf16[48,2048]{1,0:T(8,128)(2,1)S(1)}, bf16[48,2048]{1,0:T(8,128)(2,1)S(1)}, u32[]{:S(2)}, u32[]{:S(2)}) %collective-permute-start.47) | collective-permute-done | bytes 196640 | tf_op jit(solution)/shard_map/ppermute | solution.py:43
  494.2 5.8 %all-to-all-start.6 = ((bf16[8,96,128]{2,1,0:T(8,128)(2,1)}), bf16[8,96,128]{2,1,0:T(8,128)(2,1)S(1)}, u32[]{:S(2)}, u32[]{:S(2)}) async-start(bf16[8,96,128]{2,1,0:T(8,128)(2,1)} %broadcast_in_dim.35), calls=%async_computation.6 | async-start | bytes 393216 | tf_op jit(solution)/shard_map/all_to_all | solution.py:1150
  503.5 9.7 %unpack_gradients.1 = (f32[4,176,2048]{2,1,0:T(8,128)}, f32[4,176,2048]{2,1,0:T(8,128)}, f32[4,176,2048]{2,1,0:T(8,128)}) custom-call(s32[1]{0:T(128)} %bitcast.x_ref, bf16[96,2048]{1,0:T(8,128)(2,1)} %get-tuple-element.199.refs_0_, bf16[96,2048]{1,0:T(8,128)(2,1)} %copy-done.24, bf16[96,2048]{1,0:T(8,128)(2,1)} %collective-permute-done.22.refs_2_, ...), custom_call_target="tpu_custom_call" | custom-call | bytes 425984 | tf_op jit(solution)/shard_map/unpack_gradients/pallas_call | solution.py:183
  (313 shorter events, 198.2 us)
Async XLA Ops:
  19.3 19.3 %collective-permute-start.1 = (bf16[192,576]{1,0:T(8,128)(2,1)}, bf16[192,576]{1,0:T(8,128)(2,1)}, u32[]{:S(2)}, u32[]{:S(2)}) collective-permute-start(bf16[192,576]{1,0:T(8,128)(2,1)} %get-tuple-element.302), channel_id=1, source_target_pairs={{0,16},{8,24},{16,0},{24,8},{1,17},{9,25},{17,1},{25,9},{2,18},{10... | collective-permute-start | bytes 663560 | tf_op jit(solution)/shard_map/ppermute | solution.py:43
  23.4 16.1 %collective-permute-start.2 = (bf16[192,576]{1,0:T(8,128)(2,1)}, bf16[192,576]{1,0:T(8,128)(2,1)}, u32[]{:S(2)}, u32[]{:S(2)}) collective-permute-start(bf16[192,576]{1,0:T(8,128)(2,1)} %get-tuple-element.302), channel_id=1, source_target_pairs={{0,24},{8,0},{16,8},{24,16},{1,25},{9,1},{17,9},{25,17},{2,26},{10... | collective-permute-start | bytes 663560 | tf_op jit(solution)/shard_map/ppermute | solution.py:43
  25.7 38.4 %collective-permute-start.4 = (bf16[208,2048]{1,0:T(8,128)(2,1)}, bf16[208,2048]{1,0:T(8,128)(2,1)}, u32[]{:S(2)}, u32[]{:S(2)}) collective-permute-start(bf16[208,2048]{1,0:T(8,128)(2,1)} %get-tuple-element.118), channel_id=1, source_target_pairs={{0,2},{2,4},{4,6},{6,0},{1,3},{3,5},{5,7},{7,1},{8,10},{10,12},{12... | collective-permute-start | bytes 2555912 | tf_op jit(solution)/shard_map/ppermute | solution.py:43
  26.9 38.5 %collective-permute-start.5 = (bf16[208,2048]{1,0:T(8,128)(2,1)}, bf16[208,2048]{1,0:T(8,128)(2,1)}, u32[]{:S(2)}, u32[]{:S(2)}) collective-permute-start(bf16[208,2048]{1,0:T(8,128)(2,1)} %get-tuple-element.119), channel_id=1, source_target_pairs={{0,4},{2,6},{4,0},{6,2},{1,5},{3,7},{5,1},{7,3},{8,12},{10,14},{12... | collective-permute-start | bytes 2555912 | tf_op jit(solution)/shard_map/ppermute | solution.py:43
  35.0 30.9 %collective-permute-start.6 = (bf16[208,2048]{1,0:T(8,128)(2,1)}, bf16[208,2048]{1,0:T(8,128)(2,1)}, u32[]{:S(2)}, u32[]{:S(2)}) collective-permute-start(bf16[208,2048]{1,0:T(8,128)(2,1)} %get-tuple-element.120), channel_id=1, source_target_pairs={{0,6},{2,0},{4,2},{6,4},{1,7},{3,1},{5,3},{7,5},{8,14},{10,8},{12,... | collective-permute-start | bytes 2555912 | tf_op jit(solution)/shard_map/ppermute | solution.py:43
  115.5 65.1 %all-to-all-start = ((bf16[16,48,2176]{2,1,0:T(8,128)(2,1)}), bf16[16,48,2176]{2,1,0:T(8,128)(2,1)}, u32[]{:S(2)}, u32[]{:S(2)}) async-start(bf16[16,48,2176]{2,1,0:T(8,128)(2,1)} %bitcast.162), calls=%async_computation | async-start | bytes 6684672 | tf_op jit(solution)/shard_map/all_to_all | solution.py:47
  120.7 59.5 %collective-permute-start.15 = (bf16[320,2048]{1,0:T(8,128)(2,1)}, bf16[320,2048]{1,0:T(8,128)(2,1)}, u32[]{:S(2)}, u32[]{:S(2)}) collective-permute-start(bf16[320,2048]{1,0:T(8,128)(2,1)} %get-tuple-element.126), channel_id=1, source_target_pairs={{0,2},{2,4},{4,6},{6,0},{1,3},{3,5},{5,7},{7,1},{8,10},{10,12},{12... | collective-permute-start | bytes 3932168 | tf_op jit(solution)/shard_map/ppermute | solution.py:43
  120.8 59.5 %collective-permute-start.16 = (bf16[320,2048]{1,0:T(8,128)(2,1)}, bf16[320,2048]{1,0:T(8,128)(2,1)}, u32[]{:S(2)}, u32[]{:S(2)}) collective-permute-start(bf16[320,2048]{1,0:T(8,128)(2,1)} %get-tuple-element.128), channel_id=1, source_target_pairs={{0,4},{2,6},{4,0},{6,2},{1,5},{3,7},{5,1},{7,3},{8,12},{10,14},{12... | collective-permute-start | bytes 3932168 | tf_op jit(solution)/shard_map/ppermute | solution.py:43
  122.3 58.2 %collective-permute-start.17 = (bf16[320,2048]{1,0:T(8,128)(2,1)}, bf16[320,2048]{1,0:T(8,128)(2,1)}, u32[]{:S(2)}, u32[]{:S(2)}) collective-permute-start(bf16[320,2048]{1,0:T(8,128)(2,1)} %get-tuple-element.130), channel_id=1, source_target_pairs={{0,6},{2,0},{4,2},{6,4},{1,7},{3,1},{5,3},{7,5},{8,14},{10,8},{12,... | collective-permute-start | bytes 3932168 | tf_op jit(solution)/shard_map/ppermute | solution.py:43
  218.3 33.8 %all-to-all-start.1 = ((bf16[16,48,1152]{2,1,0:T(8,128)(2,1)}), bf16[16,48,1152]{2,1,0:T(8,128)(2,1)}, u32[]{:S(2)}, u32[]{:S(2)}) async-start(bf16[16,48,1152]{2,1,0:T(8,128)(2,1)} %bitcast.158), calls=%async_computation.1 | async-start | bytes 3538944 | tf_op jit(solution)/shard_map/all_to_all | solution.py:47
  224.9 249.8 %reduce-scatter.2.cloned.1.call-start = ((), (), s32[]{:S(2)}) async-start(), calls=%async_computation.10 | async-start | bytes 5013504 | tf_op jit(solution)/shard_map/reduce_scatter | solution.py:1042
  238.5 19.5 %collective-permute-start.21 = (bf16[96,2048]{1,0:T(8,128)(2,1)}, bf16[96,2048]{1,0:T(8,128)(2,1)S(1)}, u32[]{:S(2)}, u32[]{:S(2)}) collective-permute-start(bf16[96,2048]{1,0:T(8,128)(2,1)} %get-tuple-element.148), channel_id=1, source_target_pairs={{0,6},{2,0},{4,2},{6,4},{1,7},{3,1},{5,3},{7,5},{8,14},{10,8},{12,... | collective-permute-start | bytes 1179656 | tf_op jit(solution)/shard_map/ppermute | solution.py:43
  240.6 17.4 %collective-permute-start.22 = (bf16[96,2048]{1,0:T(8,128)(2,1)}, bf16[96,2048]{1,0:T(8,128)(2,1)}, u32[]{:S(2)}, u32[]{:S(2)}) collective-permute-start(bf16[96,2048]{1,0:T(8,128)(2,1)} %get-tuple-element.149), channel_id=1, source_target_pairs={{0,4},{2,6},{4,0},{6,2},{1,5},{3,7},{5,1},{7,3},{8,12},{10,14},{12... | collective-permute-start | bytes 1179656 | tf_op jit(solution)/shard_map/ppermute | solution.py:43
  240.6 20.6 %collective-permute-start.23 = (bf16[96,2048]{1,0:T(8,128)(2,1)}, bf16[96,2048]{1,0:T(8,128)(2,1)}, u32[]{:S(2)}, u32[]{:S(2)}) collective-permute-start(bf16[96,2048]{1,0:T(8,128)(2,1)} %get-tuple-element.150), channel_id=1, source_target_pairs={{0,2},{2,4},{4,6},{6,0},{1,3},{3,5},{5,7},{7,1},{8,10},{10,12},{12... | collective-permute-start | bytes 1179656 | tf_op jit(solution)/shard_map/ppermute | solution.py:43
  273.3 56.1 %all-to-all-start.2 = ((bf16[16,48,1024]{2,1,0:T(8,128)(2,1)}), bf16[16,48,1024]{2,1,0:T(8,128)(2,1)}, u32[]{:S(2)}, u32[]{:S(2)}) async-start(bf16[16,48,1024]{2,1,0:T(8,128)(2,1)} %bitcast.159), calls=%async_computation.2 | async-start | bytes 3145728 | tf_op jit(solution)/shard_map/all_to_all | solution.py:47
  304.4 21.8 %collective-permute-start.32 = (bf16[112,2048]{1,0:T(8,128)(2,1)}, bf16[112,2048]{1,0:T(8,128)(2,1)}, u32[]{:S(2)}, u32[]{:S(2)}) collective-permute-start(bf16[112,2048]{1,0:T(8,128)(2,1)} %get-tuple-element.167), channel_id=1, source_target_pairs={{0,6},{2,0},{4,2},{6,4},{1,7},{3,1},{5,3},{7,5},{8,14},{10,8},{12,... | collective-permute-start | bytes 1376264 | tf_op jit(solution)/shard_map/ppermute | solution.py:43
  305.7 20.5 %collective-permute-start.33 = (bf16[112,2048]{1,0:T(8,128)(2,1)}, bf16[112,2048]{1,0:T(8,128)(2,1)}, u32[]{:S(2)}, u32[]{:S(2)}) collective-permute-start(bf16[112,2048]{1,0:T(8,128)(2,1)} %get-tuple-element.169), channel_id=1, source_target_pairs={{0,4},{2,6},{4,0},{6,2},{1,5},{3,7},{5,1},{7,3},{8,12},{10,14},{12... | collective-permute-start | bytes 1376264 | tf_op jit(solution)/shard_map/ppermute | solution.py:43
  305.8 23.6 %collective-permute-start.34 = (bf16[112,2048]{1,0:T(8,128)(2,1)}, bf16[112,2048]{1,0:T(8,128)(2,1)}, u32[]{:S(2)}, u32[]{:S(2)}) collective-permute-start(bf16[112,2048]{1,0:T(8,128)(2,1)} %get-tuple-element.171), channel_id=1, source_target_pairs={{0,2},{2,4},{4,6},{6,0},{1,3},{3,5},{5,7},{7,1},{8,10},{10,12},{12... | collective-permute-start | bytes 1376264 | tf_op jit(solution)/shard_map/ppermute | solution.py:43
  339.2 20.8 %all-to-all-start.3 = ((bf16[16,48,576]{2,1,0:T(8,128)(2,1)}), bf16[16,48,576]{2,1,0:T(8,128)(2,1)}, u32[]{:S(2)}, u32[]{:S(2)}) async-start(bf16[16,48,576]{2,1,0:T(8,128)(2,1)} %bitcast.161), calls=%async_computation.3 | async-start | bytes 1966080 | tf_op jit(solution)/shard_map/all_to_all | solution.py:1070
  348.9 28.8 %collective-permute-start.37 = (bf16[48,2048]{1,0:T(8,128)(2,1)}, bf16[48,2048]{1,0:T(8,128)(2,1)S(1)}, u32[]{:S(2)}, u32[]{:S(2)}) collective-permute-start(bf16[48,2048]{1,0:T(8,128)(2,1)} %get-tuple-element.309), channel_id=1, source_target_pairs={{0,2},{2,4},{4,6},{6,0},{1,3},{3,5},{5,7},{7,1},{8,10},{10,12},{12... | collective-permute-start | bytes 589832 | tf_op jit(solution)/shard_map/ppermute | solution.py:43
  350.4 28.8 %collective-permute-start.39 = (bf16[48,2048]{1,0:T(8,128)(2,1)}, bf16[48,2048]{1,0:T(8,128)(2,1)S(1)}, u32[]{:S(2)}, u32[]{:S(2)}) collective-permute-start(bf16[48,2048]{1,0:T(8,128)(2,1)} %get-tuple-element.310), channel_id=1, source_target_pairs={{0,6},{2,0},{4,2},{6,4},{1,7},{3,1},{5,3},{7,5},{8,14},{10,8},{12,... | collective-permute-start | bytes 589832 | tf_op jit(solution)/shard_map/ppermute | solution.py:43
  351.8 27.4 %collective-permute-start.38 = (bf16[48,2048]{1,0:T(8,128)(2,1)S(1)}, bf16[48,2048]{1,0:T(8,128)(2,1)}, u32[]{:S(2)}, u32[]{:S(2)}) collective-permute-start(bf16[48,2048]{1,0:T(8,128)(2,1)S(1)} %get-tuple-element.311), channel_id=1, source_target_pairs={{0,4},{2,6},{4,0},{6,2},{1,5},{3,7},{5,1},{7,3},{8,12},{10,14},{12... | collective-permute-start | bytes 589832 | tf_op jit(solution)/shard_map/ppermute | solution.py:43
  353.4 39.5 %collective-permute-start.40 = (bf16[80,2048]{1,0:T(8,128)(2,1)}, bf16[80,2048]{1,0:T(8,128)(2,1)}, u32[]{:S(2)}, u32[]{:S(2)}) collective-permute-start(bf16[80,2048]{1,0:T(8,128)(2,1)} %get-tuple-element.181), channel_id=1, source_target_pairs={{0,6},{2,0},{4,2},{6,4},{1,7},{3,1},{5,3},{7,5},{8,14},{10,8},{12,... | collective-permute-start | bytes 983048 | tf_op jit(solution)/shard_map/ppermute | solution.py:43
  354.3 38.6 %collective-permute-start.41 = (bf16[80,2048]{1,0:T(8,128)(2,1)}, bf16[80,2048]{1,0:T(8,128)(2,1)}, u32[]{:S(2)}, u32[]{:S(2)}) collective-permute-start(bf16[80,2048]{1,0:T(8,128)(2,1)} %get-tuple-element.183), channel_id=1, source_target_pairs={{0,4},{2,6},{4,0},{6,2},{1,5},{3,7},{5,1},{7,3},{8,12},{10,14},{12... | collective-permute-start | bytes 983048 | tf_op jit(solution)/shard_map/ppermute | solution.py:43
  364.6 17.4 %all-to-all-start.4 = ((bf16[8,48,72]{2,1,0:T(8,128)(2,1)}), bf16[8,48,72]{2,1,0:T(8,128)(2,1)S(1)}, u32[]{:S(2)}, u32[]{:S(2)}) async-start(bf16[8,48,72]{2,1,0:T(8,128)(2,1)} %bitcast.145), calls=%async_computation.4 | async-start | bytes 196608 | tf_op jit(solution)/shard_map/all_to_all | solution.py:1090
  392.9 89.7 %all-to-all-start.5 = ((bf16[16,144,768]{2,1,0:T(8,128)(2,1)}), bf16[16,144,768]{2,1,0:T(8,128)(2,1)}, u32[]{:S(2)}, u32[]{:S(2)}) async-start(bf16[16,144,768]{2,1,0:T(8,128)(2,1)} %pad_maximum_fusion), calls=%async_computation.5 | async-start | bytes 7077888 | tf_op jit(solution)/shard_map/all_to_all | solution.py:47
  397.9 81.2 %all-gather.5.cloned.1.call-start = ((), (), s32[]{:S(2)}) async-start(), calls=%async_computation.9 | async-start | bytes 1769472 | tf_op jit(solution)/shard_map/all_gather | solution.py:86
  399.8 115.8 %all-gather.3.cloned.1.call-start = ((), (), s32[]{:S(2)}) async-start(), calls=%async_computation.8 | async-start | bytes 1769472 | tf_op jit(solution)/shard_map/all_gather | solution.py:86
  406.5 29.5 %collective-permute-start.44 = (bf16[240,2048]{1,0:T(8,128)(2,1)S(1)}, bf16[240,2048]{1,0:T(8,128)(2,1)S(1)}, u32[]{:S(2)}, u32[]{:S(2)}) collective-permute-start(bf16[240,2048]{1,0:T(8,128)(2,1)S(1)} %copy-done.45), channel_id=1, source_target_pairs={{0,6},{2,0},{4,2},{6,4},{1,7},{3,1},{5,3},{7,5},{8,14},{10,8},{12,... | collective-permute-start | bytes 2949128 | tf_op jit(solution)/shard_map/ppermute | solution.py:43
  409.1 27.9 %collective-permute-start.45 = (bf16[240,2048]{1,0:T(8,128)(2,1)S(1)}, bf16[240,2048]{1,0:T(8,128)(2,1)S(1)}, u32[]{:S(2)}, u32[]{:S(2)}) collective-permute-start(bf16[240,2048]{1,0:T(8,128)(2,1)S(1)} %copy-done.44), channel_id=1, source_target_pairs={{0,4},{2,6},{4,0},{6,2},{1,5},{3,7},{5,1},{7,3},{8,12},{10,14},{12... | collective-permute-start | bytes 2949128 | tf_op jit(solution)/shard_map/ppermute | solution.py:43
  410.3 50.9 %collective-permute-start.46 = (bf16[240,2048]{1,0:T(8,128)(2,1)S(1)}, bf16[240,2048]{1,0:T(8,128)(2,1)S(1)}, u32[]{:S(2)}, u32[]{:S(2)}) collective-permute-start(bf16[240,2048]{1,0:T(8,128)(2,1)S(1)} %copy-done.43), channel_id=1, source_target_pairs={{0,2},{2,4},{4,6},{6,0},{1,3},{3,5},{5,7},{7,1},{8,10},{10,12},{12... | collective-permute-start | bytes 2949128 | tf_op jit(solution)/shard_map/ppermute | solution.py:43
  494.2 19.0 %all-to-all-start.6 = ((bf16[8,96,128]{2,1,0:T(8,128)(2,1)}), bf16[8,96,128]{2,1,0:T(8,128)(2,1)S(1)}, u32[]{:S(2)}, u32[]{:S(2)}) async-start(bf16[8,96,128]{2,1,0:T(8,128)(2,1)} %broadcast_in_dim.35), calls=%async_computation.6 | async-start | bytes 393216 | tf_op jit(solution)/shard_map/all_to_all | solution.py:1150
  (75 other events, 611.6 us)
Sparse Core Ops, SparseCore 0:
  262.2 98.1 reduce-scatter.1
Sparse Core Ops, SparseCore 1:
  400.7 63.5 all-gather.4
  474.8 26.9 all-gather.2
where the time goes:
time: 533 us; the launch traced here: 526 us
  waiting for transfers between devices  168 us (32%)
  Pallas kernels  137 us (26%)
  starting transfers between devices  93.5 us (18%)
  other arithmetic  65.3 us (12%)
  local copies, waits for them, and re-layouts  38.5 us (7%)
  between operations  17.9 us (3%)
  matrix products  6.17 us (1%)
    ppermute x39, waiting for transfers between devices, shift(): lax.ppermute(block, axis, [(i, (i + step) % RING) for i in range(RING)])  144 us
    ppermute x39, starting transfers between devices, shift(): lax.ppermute(block, axis, [(i, (i + step) % RING) for i in range(RING)])  44 us
    all_to_all x4, starting transfers between devices, spread(): lax.all_to_all(block, EXPERT, split_axis=0, concat_axis=0, tiled=True)  23.4 us
    pallas_call x1, Pallas kernels, expert_pass(): pl.pallas_call(expert_kernel, grid_spec=pltpu.PrefetchScalarGridSpec(num_...  20.5 us
    unnamed x100, local copies, waits for them, and re-layouts  19.5 us
    pallas_call x1, Pallas kernels, attention_back(): pl.pallas_call(attention_back_kernel, grid_spec=pltpu.PrefetchScalarGridS...  18.7 us
    ppermute x11, waiting for transfers between devices, swap(): return lax.ppermute(block, 'c', [(0, 1), (1, 0)])  16.1 us
    pallas_call x1, Pallas kernels, shared_experts(): pl.pallas_call(shared_kernel, grid=(1,), in_specs=[whole(*arg.shape) for...  14.3 us
  transfers between devices with their start and end apart: 60, of which 28 were waited for; matrix products, arithmetic and copies ran while one was open for 16% of the time, Pallas kernels for 19%

commit v1 on v0

--- a/solution.py
+++ b/solution.py
@@ -1121,8 +1121,9 @@
         place, pick_b, after(produced, packed_sent), shared_part
     )
     layer_half = layer_keep + swap(layer_give).astype(F32)
-    home.append(send_home([after(piece, packed_sent) for piece in parts[3]]))
-    layer_total = residual + sum_ring(after(layer_half, *home[3]), "x", x)
+    layer_half, layer_sent = ring_parts(layer_half, x)
+    layer_total = residual + sum_sent(layer_half, layer_sent, "x")
+    home.append(send_home([after(piece, layer_total) for piece in parts[3]]))
     layer_out = gather_rows(layer_total.astype(BF))
     tokens_grad = gather_rows((mid_grad + input_norm_grad).astype(BF)).astype(F32)
     shared_sum = after(shared_grads, layer_total).astype(F32)
@@ -1148,7 +1149,7 @@
         [small_sum[:wide].astype(BF), vector_high, vector_low, jnp.zeros((10, 128), BF)], axis=0
     )
     all_small = lax.all_to_all(
-        jnp.broadcast_to(shared_small[None], (8, wide + 16, 128)), TENSOR, split_axis=0,
+        jnp.broadcast_to(after(shared_small, *home[3])[None], (8, wide + 16, 128)), TENSOR, split_axis=0,
         concat_axis=0, tiled=True,
     )
     expert_gate_grad, expert_up_grad, expert_down_grad = unpack(

time: 533 us -> 528 us (level)
    ppermute x39, waiting for transfers between devices: 144 us -> 131 us  [shift(): lax.ppermute(block, axis, [(i, (i + step) % RING) for i in range(RING)])]
    all_to_all x4, waiting for transfers between devices: 3.02 us -> 11.9 us  [spread(): lax.all_to_all(block, EXPERT, split_axis=0, concat_axis=0, tiled=True)]
    unnamed x100 -> x84, local copies, waits for them, and re-layouts: 19.5 us -> 18.2 us
  transfers between devices with their start and end apart: 60 -> 60, of which waited for: 28 -> 30; matrix products, arithmetic and copies ran while one was open for 16% -> 16% of each run, Pallas kernels for 19% -> 19%
where the time goes in v1:
time: 528 us; the launch traced here: 521 us
  waiting for transfers between devices  166 us (31%)
  Pallas kernels  137 us (26%)
  starting transfers between devices  91.7 us (17%)
  other arithmetic  65.5 us (12%)
  local copies, waits for them, and re-layouts  37.1 us (7%)
  between operations  17.8 us (3%)
  matrix products  6.18 us (1%)
    ppermute x39, waiting for transfers between devices, shift(): lax.ppermute(block, axis, [(i, (i + step) % RING) for i in range(RING)])  131 us
    ppermute x39, starting transfers between devices, shift(): lax.ppermute(block, axis, [(i, (i + step) % RING) for i in range(RING)])  44.2 us
    all_to_all x4, starting transfers between devices, spread(): lax.all_to_all(block, EXPERT, split_axis=0, concat_axis=0, tiled=True)  23.4 us
    pallas_call x1, Pallas kernels, expert_pass(): pl.pallas_call(expert_kernel, grid_spec=pltpu.PrefetchScalarGridSpec(num_...  20.6 us
    pallas_call x1, Pallas kernels, attention_back(): pl.pallas_call(attention_back_kernel, grid_spec=pltpu.PrefetchScalarGridS...  18.7 us
    unnamed x84, local copies, waits for them, and re-layouts  18.2 us
    ppermute x11, waiting for transfers between devices, swap(): return lax.ppermute(block, 'c', [(0, 1), (1, 0)])  18.2 us
    pallas_call x1, Pallas kernels, shared_experts(): pl.pallas_call(shared_kernel, grid=(1,), in_specs=[whole(*arg.shape) for...  14.3 us
  transfers between devices with their start and end apart: 60, of which 30 were waited for; matrix products, arithmetic and copies ran while one was open for 16% of the time, Pallas kernels for 19%

profile of v1, /device:TPU:1, one launch (start us, length us, event | category | flops | bytes accessed | tf_op | source)
XLA Modules:
  0.0 521.1 jit_solution(10522121310677564603)
XLA Ops:
  8.1 6.4 %pack_weights.1 = (bf16[208,2048]{1,0:T(8,128)(2,1)}, bf16[320,2048]{1,0:T(8,128)(2,1)}, bf16[208,2048]{1,0:T(8,128)(2,1)}, bf16[320,2048]{1,0:T(8,128)(2,1)}, b...) custom-call(s32[1]{0:T(128)} %bitcast.x_ref, bf16[4,176,2048]{2,1,0:T(8,128)(2,1)} %bitcast.149, ...), custom_call_target="tpu_custom_call" | custom-call | bytes 212992 | tf_op jit(solution)/shard_map/pack_weights/pallas_call | solution.py:156
  47.1 4.3 multiply_sine_fusion
  52.4 11.6 %attention_forward.1 = (bf16[4,48,2048]{2,1,0:T(8,128)(2,1)}, f32[4,48,2048]{2,1,0:T(8,128)}, bf16[384,256]{1,0:T(8,128)(2,1)}, bf16[1536,512]{1,0:T(8,128)(2,1)...) custom-call(s32[4]{0:T(128)} %pad_add_fusion.place_ref, ...), custom_call_target="tpu_custom_call" | custom-call | flops 46875000 | bytes 229376 | tf_op jit(solution)/shard_map/attention_forward/pallas_call | solution.py:545
  81.0 4.8 collective-permute-done.9
  96.1 5.4 %collective-permute-done.11.refs_1_ = bf16[48,2048]{1,0:T(8,128)(2,1)} collective-permute-done((bf16[48,2048]{1,0:T(8,128)(2,1)S(1)}, bf16[48,2048]{1,0:T(8,128)(2,1)}, u32[]{:S(2)}, u32[]{:S(2)}) %collective-permute-start.11) | collective-permute-done | bytes 196640 | tf_op jit(solution)/shard_map/ppermute | solution.py:43
  107.2 8.3 %gating.1 = (bf16[384,2048]{1,0:T(8,128)(2,1)}, f32[384,64]{1,0:T(8,128)}, bf16[768,2176]{1,0:T(8,128)(2,1)}) custom-call(s32[4]{0:T(128)} %pad_add_fusion.place_ref, bf16[4,48,2048]{2,1,0:T(8,128)(2,1)} %order_ring.2.mine_ref, bf16[4,48,2048]{2,1,0:T(8,128)(2,1)} %collective-permute-done.14.other_ref, bf16[2048,64]{1,0:T(8,128)(2,1)} %copy.79.router_ref, ...), custom_call_target="tpu_custom_call" | custom-call | flops 12500000 | bytes 98304 | tf_op jit(solution)/shard_map/gating/pallas_call | solution.py:810
  115.5 5.2 all-to-all-start
  123.4 14.3 %shared_experts.1 = (f32[384,2048]{1,0:T(8,128)}, f32[384,2048]{1,0:T(8,128)}, bf16[2048,1152]{1,0:T(8,128)(2,1)}) custom-call(bf16[384,2048]{1,0:T(8,128)(2,1)} %get-tuple-element.124.mixed, bf16[384,2048]{1,0:T(8,128)(2,1)} %out_grad.1, bf16[352,2048]{1,0:T(8,128)(2,1)} %bitcast.167, bf16[352,2048]{1,0:T(8,128)(2,1)} %bitcast.168, bf16[352,2048]{1,0:T(8,128)(2,1)} %down_w.1), custom_call_target="tpu_custom_call" | custom-call | flops 77856768 | bytes 294912 | tf_op jit(solution)/shard_map/shared_experts/pallas_call | solution.py:424
  137.7 42.5 %collective-permute-done.15.q1.p1 = bf16[320,2048]{1,0:T(8,128)(2,1)} collective-permute-done((bf16[320,2048]{1,0:T(8,128)(2,1)}, bf16[320,2048]{1,0:T(8,128)(2,1)}, u32[]{:S(2)}, u32[]{:S(2)}) %collective-permute-start.15) | collective-permute-done | bytes 1310752 | tf_op jit(solution)/shard_map/ppermute | solution.py:43
  182.6 5.8 %collective-permute-done.18.other_ref.grad_other_ref.refs_4_.refs_6_ = bf16[768,2176]{1,0:T(8,128)(2,1)S(1)} collective-permute-done((bf16[768,2176]{1,0:T(8,128)(2,1)}, bf16[768,2176]{1,0:T(8,128)(2,1)S(1)}, u32[]{:S(2)}, u32[]{:S(2)}) %collective-permute-start.18) | collective-permute-done | bytes 3342368 | tf_op jit(solution)/shard_map/ppermute | solution.py:39
  190.1 20.6 %expert_pass.1 = (bf16[768,704]{1,0:T(8,128)(2,1)}, bf16[768,704]{1,0:T(8,128)(2,1)}, bf16[768,704]{1,0:T(8,128)(2,1)}, bf16[768,704]{1,0:T(8,128)(2,1)}, f32[76...) custom-call(s32[4]{0:T(128)} %pad_add_fusion.place_ref, ...), custom_call_target="tpu_custom_call" | custom-call | flops 173015040 | bytes 393216 | tf_op jit(solution)/shard_map/expert_pass/pallas_call | solution.py:292
  218.3 6.6 %all-to-all-start.1 = ((bf16[16,48,1152]{2,1,0:T(8,128)(2,1)}), bf16[16,48,1152]{2,1,0:T(8,128)(2,1)}, u32[]{:S(2)}, u32[]{:S(2)}) async-start(bf16[16,48,1152]{2,1,0:T(8,128)(2,1)} %bitcast.158), calls=%async_computation.1 | async-start | bytes 3538944 | tf_op jit(solution)/shard_map/all_to_all | solution.py:47
  225.0 13.5 %weight_grads.1 = (bf16[96,2048]{1,0:T(8,128)(2,1)}, bf16[96,2048]{1,0:T(8,128)(2,1)}, bf16[96,2048]{1,0:T(8,128)(2,1)}, bf16[96,2048]{1,0:T(8,128)(2,1)}, bf16[...) custom-call(s32[4]{0:T(128)} %pad_add_fusion.place_ref, ...), custom_call_target="tpu_custom_call" | custom-call | flops 103809024 | bytes 294912 | tf_op jit(solution)/shard_map/weight_grads/pallas_call | solution.py:371
  241.3 7.8 %produce.1 = (f32[768,1024]{1,0:T(8,128)}, bf16[768,1024]{1,0:T(8,128)(2,1)}) custom-call(s32[4]{0:T(128)} %pad_add_fusion.place_ref, bf16[768,704]{1,0:T(8,128)(2,1)} %get-tuple-element.141.act_ref, bf16[768,2176]{1,0:T(8,128)(2,1)} %bitcast.19.mine_ref.grad_mine_ref.gate_ref.refs_3_.refs_5_, bf16[4,176,2048]{2,1,0:T(8,128)(2,1)} %own_down.3, ...), custom_call_target="tpu_custom_call" | custom-call | flops 34603008 | bytes 147456 | tf_op jit(solution)/shard_map/produce/pallas_call | solution.py:324
  252.1 5.9 %combine_rows.2 = (bf16[4,48,2176]{2,1,0:T(8,128)(2,1)}, f32[4,48,2176]{2,1,0:T(8,128)}) custom-call(s32[4]{0:T(128)} %pad_add_fusion.place_ref, bf16[768,384]{1,0:T(8,128)(2,1)} %fusion.4.pick_ref, bf16[768,1152]{1,0:T(8,128)(2,1)} %bitcast.23.returned_ref, f32[384,2048]{1,0:T(8,128)} %get-tuple-element.145.shared_ref), custom_call_target="tpu_custom_call" | custom-call | flops 10937500 | bytes 131072 | tf_op jit(solution)/shard_map/combine_rows/pallas_call | solution.py:729
  273.4 6.7 %all-to-all-start.2 = ((bf16[16,48,1024]{2,1,0:T(8,128)(2,1)}), bf16[16,48,1024]{2,1,0:T(8,128)(2,1)}, u32[]{:S(2)}, u32[]{:S(2)}) async-start(bf16[16,48,1024]{2,1,0:T(8,128)(2,1)} %bitcast.159), calls=%async_computation.2 | async-start | bytes 3145728 | tf_op jit(solution)/shard_map/all_to_all | solution.py:47
  290.4 4.4 collective-permute-done.30.refs_3_
  295.4 6.0 %collective-permute-done.28.refs_1_ = bf16[48,2176]{1,0:T(8,128)(2,1)} collective-permute-done((bf16[48,2176]{1,0:T(8,128)(2,1)S(1)}, bf16[48,2176]{1,0:T(8,128)(2,1)}, u32[]{:S(2)}, u32[]{:S(2)}) %collective-permute-start.28) | collective-permute-done | bytes 208928 | tf_op jit(solution)/shard_map/ppermute | solution.py:43
  307.5 18.7 %attention_backward.1 = (bf16[4,4,48,576]{3,2,1,0:T(8,128)(2,1)}, f32[4,4,48,576]{3,2,1,0:T(8,128)}, bf16[1536,512]{1,0:T(8,128)(2,1)}, bf16[384,384]{1,0:T(8,12...) custom-call(s32[4]{0:T(128)} %pad_add_fusion.place_ref, ...), custom_call_target="tpu_custom_call" | custom-call | flops 62500000 | bytes 262144 | tf_op jit(solution)/shard_map/attention_backward/pallas_call | solution.py:652
  339.3 4.5 all-to-all-start.3
  355.6 4.5 all-to-all-done.3
  364.7 5.8 %all-to-all-start.4 = ((bf16[8,48,72]{2,1,0:T(8,128)(2,1)}), bf16[8,48,72]{2,1,0:T(8,128)(2,1)S(1)}, u32[]{:S(2)}, u32[]{:S(2)}) async-start(bf16[8,48,72]{2,1,0:T(8,128)(2,1)} %bitcast.145), calls=%async_computation.4 | async-start | bytes 196608 | tf_op jit(solution)/shard_map/all_to_all | solution.py:1090
  370.5 6.8 %projection_grads.1 = bf16[2048,768]{1,0:T(8,128)(2,1)} custom-call(bf16[384,2048]{1,0:T(8,128)(2,1)} %copy-done.2, bf16[384,2176]{1,0:T(8,128)(2,1)} %get-tuple-element.158.branch, bf16[1536,512]{1,0:T(8,128)(2,1)} %get-tuple-element.154.compressed_ref.compressed, bf16[384,384]{1,0:T(8,128)(2,1)} %get-tuple-element.159.query_grad, ...), custom_call_target="tpu_custom_call" | custom-call | flops 31250000 | bytes 163840 | tf_op jit(solution)/shard_map/projection_grads/pallas_call | solution.py:689
  388.4 4.1 pad_maximum_fusion
  393.0 5.0 all-to-all-start.5
  400.0 5.7 %combine_rows.3 = (bf16[4,48,2048]{2,1,0:T(8,128)(2,1)}, f32[4,48,2048]{2,1,0:T(8,128)}) custom-call(s32[4]{0:T(128)} %pad_add_fusion.place_ref, bf16[768,384]{1,0:T(8,128)(2,1)} %fusion.4.pick_ref, bf16[768,1024]{1,0:T(8,128)(2,1)} %bitcast.28.returned_ref, f32[384,2048]{1,0:T(8,128)} %get-tuple-element.125.shared_ref), custom_call_target="tpu_custom_call" | custom-call | flops 10937500 | bytes 131072 | tf_op jit(solution)/shard_map/combine_rows/pallas_call | solution.py:729
  416.7 6.0 %collective-permute-done.44 = bf16[48,2048]{1,0:T(8,128)(2,1)S(1)} collective-permute-done((bf16[48,2048]{1,0:T(8,128)(2,1)S(1)}, bf16[48,2048]{1,0:T(8,128)(2,1)S(1)}, u32[]{:S(2)}, u32[]{:S(2)}) %collective-permute-start.44) | collective-permute-done | bytes 196640 | tf_op jit(solution)/shard_map/ppermute | solution.py:43
  422.7 7.9 %collective-permute-done.45 = bf16[48,2048]{1,0:T(8,128)(2,1)} collective-permute-done((bf16[48,2048]{1,0:T(8,128)(2,1)S(1)}, bf16[48,2048]{1,0:T(8,128)(2,1)}, u32[]{:S(2)}, u32[]{:S(2)}) %collective-permute-start.45) | collective-permute-done | bytes 196640 | tf_op jit(solution)/shard_map/ppermute | solution.py:43
  442.4 8.9 %all-to-all-done.5 = bf16[16,144,768]{2,1,0:T(8,128)(2,1)} async-done(((bf16[16,144,768]{2,1,0:T(8,128)(2,1)}), bf16[16,144,768]{2,1,0:T(8,128)(2,1)}, u32[]{:S(2)}, u32[]{:S(2)}) %all-to-all-start.5) | async-done | bytes 3538976 | tf_op jit(solution)/shard_map/all_to_all | solution.py:47
  460.7 4.8 collective-permute-done.47.refs_13_
  465.5 24.9 %collective-permute-done.49.refs_15_ = bf16[240,2048]{1,0:T(8,128)(2,1)} collective-permute-done((bf16[240,2048]{1,0:T(8,128)(2,1)}, bf16[240,2048]{1,0:T(8,128)(2,1)}, u32[]{:S(2)}, u32[]{:S(2)}) %collective-permute-start.49) | collective-permute-done | bytes 983072 | tf_op jit(solution)/shard_map/ppermute | solution.py:43
  498.5 9.7 %unpack_gradients.1 = (f32[4,176,2048]{2,1,0:T(8,128)}, f32[4,176,2048]{2,1,0:T(8,128)}, f32[4,176,2048]{2,1,0:T(8,128)}) custom-call(s32[1]{0:T(128)} %bitcast.x_ref, bf16[96,2048]{1,0:T(8,128)(2,1)} %get-tuple-element.199.refs_0_, bf16[96,2048]{1,0:T(8,128)(2,1)} %copy-done.19, bf16[96,2048]{1,0:T(8,128)(2,1)} %collective-permute-done.22.refs_2_, ...), custom_call_target="tpu_custom_call" | custom-call | bytes 425984 | tf_op jit(solution)/shard_map/unpack_gradients/pallas_call | solution.py:183
  (296 shorter events, 205.8 us)
Async XLA Ops:
  19.3 19.3 %collective-permute-start.1 = (bf16[192,576]{1,0:T(8,128)(2,1)}, bf16[192,576]{1,0:T(8,128)(2,1)}, u32[]{:S(2)}, u32[]{:S(2)}) collective-permute-start(bf16[192,576]{1,0:T(8,128)(2,1)} %get-tuple-element.302), channel_id=1, source_target_pairs={{0,16},{8,24},{16,0},{24,8},{1,17},{9,25},{17,1},{25,9},{2,18},{10... | collective-permute-start | bytes 663560 | tf_op jit(solution)/shard_map/ppermute | solution.py:43
  25.7 38.3 %collective-permute-start.4 = (bf16[208,2048]{1,0:T(8,128)(2,1)}, bf16[208,2048]{1,0:T(8,128)(2,1)}, u32[]{:S(2)}, u32[]{:S(2)}) collective-permute-start(bf16[208,2048]{1,0:T(8,128)(2,1)} %get-tuple-element.118), channel_id=1, source_target_pairs={{0,2},{2,4},{4,6},{6,0},{1,3},{3,5},{5,7},{7,1},{8,10},{10,12},{12... | collective-permute-start | bytes 2555912 | tf_op jit(solution)/shard_map/ppermute | solution.py:43
  26.9 38.5 %collective-permute-start.5 = (bf16[208,2048]{1,0:T(8,128)(2,1)}, bf16[208,2048]{1,0:T(8,128)(2,1)}, u32[]{:S(2)}, u32[]{:S(2)}) collective-permute-start(bf16[208,2048]{1,0:T(8,128)(2,1)} %get-tuple-element.119), channel_id=1, source_target_pairs={{0,4},{2,6},{4,0},{6,2},{1,5},{3,7},{5,1},{7,3},{8,12},{10,14},{12... | collective-permute-start | bytes 2555912 | tf_op jit(solution)/shard_map/ppermute | solution.py:43
  35.0 30.9 %collective-permute-start.6 = (bf16[208,2048]{1,0:T(8,128)(2,1)}, bf16[208,2048]{1,0:T(8,128)(2,1)}, u32[]{:S(2)}, u32[]{:S(2)}) collective-permute-start(bf16[208,2048]{1,0:T(8,128)(2,1)} %get-tuple-element.120), channel_id=1, source_target_pairs={{0,6},{2,0},{4,2},{6,4},{1,7},{3,1},{5,3},{7,5},{8,14},{10,8},{12,... | collective-permute-start | bytes 2555912 | tf_op jit(solution)/shard_map/ppermute | solution.py:43
  115.5 65.1 %all-to-all-start = ((bf16[16,48,2176]{2,1,0:T(8,128)(2,1)}), bf16[16,48,2176]{2,1,0:T(8,128)(2,1)}, u32[]{:S(2)}, u32[]{:S(2)}) async-start(bf16[16,48,2176]{2,1,0:T(8,128)(2,1)} %bitcast.162), calls=%async_computation | async-start | bytes 6684672 | tf_op jit(solution)/shard_map/all_to_all | solution.py:47
  120.7 59.6 %collective-permute-start.15 = (bf16[320,2048]{1,0:T(8,128)(2,1)}, bf16[320,2048]{1,0:T(8,128)(2,1)}, u32[]{:S(2)}, u32[]{:S(2)}) collective-permute-start(bf16[320,2048]{1,0:T(8,128)(2,1)} %get-tuple-element.126), channel_id=1, source_target_pairs={{0,2},{2,4},{4,6},{6,0},{1,3},{3,5},{5,7},{7,1},{8,10},{10,12},{12... | collective-permute-start | bytes 3932168 | tf_op jit(solution)/shard_map/ppermute | solution.py:43
  120.8 59.5 %collective-permute-start.16 = (bf16[320,2048]{1,0:T(8,128)(2,1)}, bf16[320,2048]{1,0:T(8,128)(2,1)}, u32[]{:S(2)}, u32[]{:S(2)}) collective-permute-start(bf16[320,2048]{1,0:T(8,128)(2,1)} %get-tuple-element.128), channel_id=1, source_target_pairs={{0,4},{2,6},{4,0},{6,2},{1,5},{3,7},{5,1},{7,3},{8,12},{10,14},{12... | collective-permute-start | bytes 3932168 | tf_op jit(solution)/shard_map/ppermute | solution.py:43
  122.4 58.3 %collective-permute-start.17 = (bf16[320,2048]{1,0:T(8,128)(2,1)}, bf16[320,2048]{1,0:T(8,128)(2,1)}, u32[]{:S(2)}, u32[]{:S(2)}) collective-permute-start(bf16[320,2048]{1,0:T(8,128)(2,1)} %get-tuple-element.130), channel_id=1, source_target_pairs={{0,6},{2,0},{4,2},{6,4},{1,7},{3,1},{5,3},{7,5},{8,14},{10,8},{12,... | collective-permute-start | bytes 3932168 | tf_op jit(solution)/shard_map/ppermute | solution.py:43
  218.3 33.8 %all-to-all-start.1 = ((bf16[16,48,1152]{2,1,0:T(8,128)(2,1)}), bf16[16,48,1152]{2,1,0:T(8,128)(2,1)}, u32[]{:S(2)}, u32[]{:S(2)}) async-start(bf16[16,48,1152]{2,1,0:T(8,128)(2,1)} %bitcast.158), calls=%async_computation.1 | async-start | bytes 3538944 | tf_op jit(solution)/shard_map/all_to_all | solution.py:47
  224.9 207.6 %reduce-scatter.2.cloned.1.call-start = ((), (), s32[]{:S(2)}) async-start(), calls=%async_computation.10 | async-start | bytes 5013504 | tf_op jit(solution)/shard_map/reduce_scatter | solution.py:1042
  238.5 19.5 %collective-permute-start.21 = (bf16[96,2048]{1,0:T(8,128)(2,1)}, bf16[96,2048]{1,0:T(8,128)(2,1)S(1)}, u32[]{:S(2)}, u32[]{:S(2)}) collective-permute-start(bf16[96,2048]{1,0:T(8,128)(2,1)} %get-tuple-element.148), channel_id=1, source_target_pairs={{0,6},{2,0},{4,2},{6,4},{1,7},{3,1},{5,3},{7,5},{8,14},{10,8},{12,... | collective-permute-start | bytes 1179656 | tf_op jit(solution)/shard_map/ppermute | solution.py:43
  240.6 17.4 %collective-permute-start.22 = (bf16[96,2048]{1,0:T(8,128)(2,1)}, bf16[96,2048]{1,0:T(8,128)(2,1)}, u32[]{:S(2)}, u32[]{:S(2)}) collective-permute-start(bf16[96,2048]{1,0:T(8,128)(2,1)} %get-tuple-element.149), channel_id=1, source_target_pairs={{0,4},{2,6},{4,0},{6,2},{1,5},{3,7},{5,1},{7,3},{8,12},{10,14},{12... | collective-permute-start | bytes 1179656 | tf_op jit(solution)/shard_map/ppermute | solution.py:43
  240.6 20.6 %collective-permute-start.23 = (bf16[96,2048]{1,0:T(8,128)(2,1)}, bf16[96,2048]{1,0:T(8,128)(2,1)}, u32[]{:S(2)}, u32[]{:S(2)}) collective-permute-start(bf16[96,2048]{1,0:T(8,128)(2,1)} %get-tuple-element.150), channel_id=1, source_target_pairs={{0,2},{2,4},{4,6},{6,0},{1,3},{3,5},{5,7},{7,1},{8,10},{10,12},{12... | collective-permute-start | bytes 1179656 | tf_op jit(solution)/shard_map/ppermute | solution.py:43
  273.4 56.1 %all-to-all-start.2 = ((bf16[16,48,1024]{2,1,0:T(8,128)(2,1)}), bf16[16,48,1024]{2,1,0:T(8,128)(2,1)}, u32[]{:S(2)}, u32[]{:S(2)}) async-start(bf16[16,48,1024]{2,1,0:T(8,128)(2,1)} %bitcast.159), calls=%async_computation.2 | async-start | bytes 3145728 | tf_op jit(solution)/shard_map/all_to_all | solution.py:47
  304.4 21.8 %collective-permute-start.32 = (bf16[112,2048]{1,0:T(8,128)(2,1)}, bf16[112,2048]{1,0:T(8,128)(2,1)}, u32[]{:S(2)}, u32[]{:S(2)}) collective-permute-start(bf16[112,2048]{1,0:T(8,128)(2,1)} %get-tuple-element.167), channel_id=1, source_target_pairs={{0,6},{2,0},{4,2},{6,4},{1,7},{3,1},{5,3},{7,5},{8,14},{10,8},{12,... | collective-permute-start | bytes 1376264 | tf_op jit(solution)/shard_map/ppermute | solution.py:43
  305.8 20.5 %collective-permute-start.33 = (bf16[112,2048]{1,0:T(8,128)(2,1)}, bf16[112,2048]{1,0:T(8,128)(2,1)}, u32[]{:S(2)}, u32[]{:S(2)}) collective-permute-start(bf16[112,2048]{1,0:T(8,128)(2,1)} %get-tuple-element.169), channel_id=1, source_target_pairs={{0,4},{2,6},{4,0},{6,2},{1,5},{3,7},{5,1},{7,3},{8,12},{10,14},{12... | collective-permute-start | bytes 1376264 | tf_op jit(solution)/shard_map/ppermute | solution.py:43
  305.9 23.6 %collective-permute-start.34 = (bf16[112,2048]{1,0:T(8,128)(2,1)}, bf16[112,2048]{1,0:T(8,128)(2,1)}, u32[]{:S(2)}, u32[]{:S(2)}) collective-permute-start(bf16[112,2048]{1,0:T(8,128)(2,1)} %get-tuple-element.171), channel_id=1, source_target_pairs={{0,2},{2,4},{4,6},{6,0},{1,3},{3,5},{5,7},{7,1},{8,10},{10,12},{12... | collective-permute-start | bytes 1376264 | tf_op jit(solution)/shard_map/ppermute | solution.py:43
  339.3 20.8 %all-to-all-start.3 = ((bf16[16,48,576]{2,1,0:T(8,128)(2,1)}), bf16[16,48,576]{2,1,0:T(8,128)(2,1)}, u32[]{:S(2)}, u32[]{:S(2)}) async-start(bf16[16,48,576]{2,1,0:T(8,128)(2,1)} %bitcast.161), calls=%async_computation.3 | async-start | bytes 1966080 | tf_op jit(solution)/shard_map/all_to_all | solution.py:1070
  349.0 28.8 %collective-permute-start.37 = (bf16[48,2048]{1,0:T(8,128)(2,1)}, bf16[48,2048]{1,0:T(8,128)(2,1)S(1)}, u32[]{:S(2)}, u32[]{:S(2)}) collective-permute-start(bf16[48,2048]{1,0:T(8,128)(2,1)} %get-tuple-element.309), channel_id=1, source_target_pairs={{0,2},{2,4},{4,6},{6,0},{1,3},{3,5},{5,7},{7,1},{8,10},{10,12},{12... | collective-permute-start | bytes 589832 | tf_op jit(solution)/shard_map/ppermute | solution.py:43
  350.5 28.8 %collective-permute-start.39 = (bf16[48,2048]{1,0:T(8,128)(2,1)}, bf16[48,2048]{1,0:T(8,128)(2,1)S(1)}, u32[]{:S(2)}, u32[]{:S(2)}) collective-permute-start(bf16[48,2048]{1,0:T(8,128)(2,1)} %get-tuple-element.310), channel_id=1, source_target_pairs={{0,6},{2,0},{4,2},{6,4},{1,7},{3,1},{5,3},{7,5},{8,14},{10,8},{12,... | collective-permute-start | bytes 589832 | tf_op jit(solution)/shard_map/ppermute | solution.py:43
  351.9 27.4 %collective-permute-start.38 = (bf16[48,2048]{1,0:T(8,128)(2,1)S(1)}, bf16[48,2048]{1,0:T(8,128)(2,1)}, u32[]{:S(2)}, u32[]{:S(2)}) collective-permute-start(bf16[48,2048]{1,0:T(8,128)(2,1)S(1)} %get-tuple-element.311), channel_id=1, source_target_pairs={{0,4},{2,6},{4,0},{6,2},{1,5},{3,7},{5,1},{7,3},{8,12},{10,14},{12... | collective-permute-start | bytes 589832 | tf_op jit(solution)/shard_map/ppermute | solution.py:43
  353.5 39.5 %collective-permute-start.40 = (bf16[80,2048]{1,0:T(8,128)(2,1)}, bf16[80,2048]{1,0:T(8,128)(2,1)}, u32[]{:S(2)}, u32[]{:S(2)}) collective-permute-start(bf16[80,2048]{1,0:T(8,128)(2,1)} %get-tuple-element.181), channel_id=1, source_target_pairs={{0,6},{2,0},{4,2},{6,4},{1,7},{3,1},{5,3},{7,5},{8,14},{10,8},{12,... | collective-permute-start | bytes 983048 | tf_op jit(solution)/shard_map/ppermute | solution.py:43
  354.4 38.6 %collective-permute-start.41 = (bf16[80,2048]{1,0:T(8,128)(2,1)}, bf16[80,2048]{1,0:T(8,128)(2,1)}, u32[]{:S(2)}, u32[]{:S(2)}) collective-permute-start(bf16[80,2048]{1,0:T(8,128)(2,1)} %get-tuple-element.183), channel_id=1, source_target_pairs={{0,4},{2,6},{4,0},{6,2},{1,5},{3,7},{5,1},{7,3},{8,12},{10,14},{12... | collective-permute-start | bytes 983048 | tf_op jit(solution)/shard_map/ppermute | solution.py:43
  364.7 17.4 %all-to-all-start.4 = ((bf16[8,48,72]{2,1,0:T(8,128)(2,1)}), bf16[8,48,72]{2,1,0:T(8,128)(2,1)S(1)}, u32[]{:S(2)}, u32[]{:S(2)}) async-start(bf16[8,48,72]{2,1,0:T(8,128)(2,1)} %bitcast.145), calls=%async_computation.4 | async-start | bytes 196608 | tf_op jit(solution)/shard_map/all_to_all | solution.py:1090
  393.0 58.3 %all-to-all-start.5 = ((bf16[16,144,768]{2,1,0:T(8,128)(2,1)}), bf16[16,144,768]{2,1,0:T(8,128)(2,1)}, u32[]{:S(2)}, u32[]{:S(2)}) async-start(bf16[16,144,768]{2,1,0:T(8,128)(2,1)} %pad_maximum_fusion), calls=%async_computation.5 | async-start | bytes 7077888 | tf_op jit(solution)/shard_map/all_to_all | solution.py:47
  398.0 40.9 %all-gather.5.cloned.1.call-start = ((), (), s32[]{:S(2)}) async-start(), calls=%async_computation.9 | async-start | bytes 1769472 | tf_op jit(solution)/shard_map/all_gather | solution.py:86
  399.9 110.8 %all-gather.3.cloned.1.call-start = ((), (), s32[]{:S(2)}) async-start(), calls=%async_computation.8 | async-start | bytes 1769472 | tf_op jit(solution)/shard_map/all_gather | solution.py:86
  414.1 16.5 %collective-permute-start.45 = (bf16[48,2048]{1,0:T(8,128)(2,1)S(1)}, bf16[48,2048]{1,0:T(8,128)(2,1)}, u32[]{:S(2)}, u32[]{:S(2)}) collective-permute-start(bf16[48,2048]{1,0:T(8,128)(2,1)S(1)} %get-tuple-element.308), channel_id=1, source_target_pairs={{0,4},{2,6},{4,0},{6,2},{1,5},{3,7},{5,1},{7,3},{8,12},{10,14},{12... | collective-permute-start | bytes 589832 | tf_op jit(solution)/shard_map/ppermute | solution.py:43
  437.0 28.5 %collective-permute-start.47 = (bf16[240,2048]{1,0:T(8,128)(2,1)}, bf16[240,2048]{1,0:T(8,128)(2,1)}, u32[]{:S(2)}, u32[]{:S(2)}) collective-permute-start(bf16[240,2048]{1,0:T(8,128)(2,1)} %get-tuple-element.193), channel_id=1, source_target_pairs={{0,6},{2,0},{4,2},{6,4},{1,7},{3,1},{5,3},{7,5},{8,14},{10,8},{12,... | collective-permute-start | bytes 2949128 | tf_op jit(solution)/shard_map/ppermute | solution.py:43
  437.6 27.9 %collective-permute-start.48 = (bf16[240,2048]{1,0:T(8,128)(2,1)}, bf16[240,2048]{1,0:T(8,128)(2,1)}, u32[]{:S(2)}, u32[]{:S(2)}) collective-permute-start(bf16[240,2048]{1,0:T(8,128)(2,1)} %get-tuple-element.195), channel_id=1, source_target_pairs={{0,4},{2,6},{4,0},{6,2},{1,5},{3,7},{5,1},{7,3},{8,12},{10,14},{12... | collective-permute-start | bytes 2949128 | tf_op jit(solution)/shard_map/ppermute | solution.py:43
  438.9 51.6 %collective-permute-start.49 = (bf16[240,2048]{1,0:T(8,128)(2,1)}, bf16[240,2048]{1,0:T(8,128)(2,1)}, u32[]{:S(2)}, u32[]{:S(2)}) collective-permute-start(bf16[240,2048]{1,0:T(8,128)(2,1)} %get-tuple-element.197), channel_id=1, source_target_pairs={{0,2},{2,4},{4,6},{6,0},{1,3},{3,5},{5,7},{7,1},{8,10},{10,12},{12... | collective-permute-start | bytes 2949128 | tf_op jit(solution)/shard_map/ppermute | solution.py:43
  491.2 17.0 %all-to-all-start.6 = ((bf16[8,96,128]{2,1,0:T(8,128)(2,1)}), bf16[8,96,128]{2,1,0:T(8,128)(2,1)S(1)}, u32[]{:S(2)}, u32[]{:S(2)}) async-start(bf16[8,96,128]{2,1,0:T(8,128)(2,1)} %broadcast_in_dim.35), calls=%async_computation.6 | async-start | bytes 393216 | tf_op jit(solution)/shard_map/all_to_all | solution.py:1151
  (66 other events, 478.0 us)
Sparse Core Ops, SparseCore 0:
  262.3 98.1 reduce-scatter.1
Sparse Core Ops, SparseCore 1:
  400.8 28.6 all-gather.4
  432.7 59.3 all-gather.2

commit v2 on v1

--- a/solution.py
+++ b/solution.py
@@ -124,7 +124,7 @@
 
 
 OUTWARD = (208, 320)
-HOMEWARD = (96, 112, 80, 240)
+HOMEWARD = (96, 112, 96, 224)
 
 
 def spans(parts):

time: 528 us -> 529 us (level)
    unnamed x84 -> x86, local copies, waits for them, and re-layouts: 18.2 us -> 19.8 us
  transfers between devices with their start and end apart: 60 -> 60, of which waited for: 30 -> 31; matrix products, arithmetic and copies ran while one was open for 16% -> 16% of each run, Pallas kernels for 19% -> 19%
where the time goes in v2:
time: 529 us; the launch traced here: 522 us
  waiting for transfers between devices  163 us (31%)
  Pallas kernels  137 us (26%)
  starting transfers between devices  93.3 us (18%)
  other arithmetic  65.2 us (12%)
  local copies, waits for them, and re-layouts  39.6 us (7%)
  between operations  17.8 us (3%)
  matrix products  6.14 us (1%)
    ppermute x39, waiting for transfers between devices, shift(): lax.ppermute(block, axis, [(i, (i + step) % RING) for i in range(RING)])  127 us
    ppermute x39, starting transfers between devices, shift(): lax.ppermute(block, axis, [(i, (i + step) % RING) for i in range(RING)])  44.2 us
    all_to_all x4, starting transfers between devices, spread(): lax.all_to_all(block, EXPERT, split_axis=0, concat_axis=0, tiled=True)  25 us
    pallas_call x1, Pallas kernels, expert_pass(): pl.pallas_call(expert_kernel, grid_spec=pltpu.PrefetchScalarGridSpec(num_...  20.6 us
    unnamed x86, local copies, waits for them, and re-layouts  19.8 us
    pallas_call x1, Pallas kernels, attention_back(): pl.pallas_call(attention_back_kernel, grid_spec=pltpu.PrefetchScalarGridS...  18.7 us
    ppermute x11, waiting for transfers between devices, swap(): return lax.ppermute(block, 'c', [(0, 1), (1, 0)])  18.2 us
    pallas_call x1, Pallas kernels, shared_experts(): pl.pallas_call(shared_kernel, grid=(1,), in_specs=[whole(*arg.shape) for...  14.3 us
  transfers between devices with their start and end apart: 60, of which 31 were waited for; matrix products, arithmetic and copies ran while one was open for 16% of the time, Pallas kernels for 19%

profile of v2, /device:TPU:1, one launch (start us, length us, event | category | flops | bytes accessed | tf_op | source)
XLA Modules:
  0.0 522.1 jit_solution(16491734463954944853)
XLA Ops:
  8.1 6.4 %pack_weights.1 = (bf16[208,2048]{1,0:T(8,128)(2,1)}, bf16[320,2048]{1,0:T(8,128)(2,1)}, bf16[208,2048]{1,0:T(8,128)(2,1)}, bf16[320,2048]{1,0:T(8,128)(2,1)}, b...) custom-call(s32[1]{0:T(128)} %bitcast.x_ref, bf16[4,176,2048]{2,1,0:T(8,128)(2,1)} %bitcast.149, ...), custom_call_target="tpu_custom_call" | custom-call | bytes 212992 | tf_op jit(solution)/shard_map/pack_weights/pallas_call | solution.py:156
  47.1 4.3 multiply_sine_fusion
  52.4 11.7 %attention_forward.1 = (bf16[4,48,2048]{2,1,0:T(8,128)(2,1)}, f32[4,48,2048]{2,1,0:T(8,128)}, bf16[384,256]{1,0:T(8,128)(2,1)}, bf16[1536,512]{1,0:T(8,128)(2,1)...) custom-call(s32[4]{0:T(128)} %pad_add_fusion.place_ref, ...), custom_call_target="tpu_custom_call" | custom-call | flops 46875000 | bytes 229376 | tf_op jit(solution)/shard_map/attention_forward/pallas_call | solution.py:545
  81.0 4.8 collective-permute-done.9
  96.1 5.4 %collective-permute-done.11.refs_1_ = bf16[48,2048]{1,0:T(8,128)(2,1)} collective-permute-done((bf16[48,2048]{1,0:T(8,128)(2,1)S(1)}, bf16[48,2048]{1,0:T(8,128)(2,1)}, u32[]{:S(2)}, u32[]{:S(2)}) %collective-permute-start.11) | collective-permute-done | bytes 196640 | tf_op jit(solution)/shard_map/ppermute | solution.py:43
  107.2 8.3 %gating.1 = (bf16[384,2048]{1,0:T(8,128)(2,1)}, f32[384,64]{1,0:T(8,128)}, bf16[768,2176]{1,0:T(8,128)(2,1)}) custom-call(s32[4]{0:T(128)} %pad_add_fusion.place_ref, bf16[4,48,2048]{2,1,0:T(8,128)(2,1)} %order_ring.2.mine_ref, bf16[4,48,2048]{2,1,0:T(8,128)(2,1)} %collective-permute-done.14.other_ref, bf16[2048,64]{1,0:T(8,128)(2,1)} %copy.79.router_ref, ...), custom_call_target="tpu_custom_call" | custom-call | flops 12500000 | bytes 98304 | tf_op jit(solution)/shard_map/gating/pallas_call | solution.py:810
  115.5 5.2 all-to-all-start
  123.4 14.3 %shared_experts.1 = (f32[384,2048]{1,0:T(8,128)}, f32[384,2048]{1,0:T(8,128)}, bf16[2048,1152]{1,0:T(8,128)(2,1)}) custom-call(bf16[384,2048]{1,0:T(8,128)(2,1)} %get-tuple-element.124.mixed, bf16[384,2048]{1,0:T(8,128)(2,1)} %out_grad.1, bf16[352,2048]{1,0:T(8,128)(2,1)} %bitcast.167, bf16[352,2048]{1,0:T(8,128)(2,1)} %bitcast.168, bf16[352,2048]{1,0:T(8,128)(2,1)} %down_w.1), custom_call_target="tpu_custom_call" | custom-call | flops 77856768 | bytes 294912 | tf_op jit(solution)/shard_map/shared_experts/pallas_call | solution.py:424
  137.7 42.5 %collective-permute-done.15.q1.p1 = bf16[320,2048]{1,0:T(8,128)(2,1)} collective-permute-done((bf16[320,2048]{1,0:T(8,128)(2,1)}, bf16[320,2048]{1,0:T(8,128)(2,1)}, u32[]{:S(2)}, u32[]{:S(2)}) %collective-permute-start.15) | collective-permute-done | bytes 1310752 | tf_op jit(solution)/shard_map/ppermute | solution.py:43
  182.6 5.8 %collective-permute-done.18.other_ref.grad_other_ref.refs_4_.refs_6_ = bf16[768,2176]{1,0:T(8,128)(2,1)S(1)} collective-permute-done((bf16[768,2176]{1,0:T(8,128)(2,1)}, bf16[768,2176]{1,0:T(8,128)(2,1)S(1)}, u32[]{:S(2)}, u32[]{:S(2)}) %collective-permute-start.18) | collective-permute-done | bytes 3342368 | tf_op jit(solution)/shard_map/ppermute | solution.py:39
  190.1 20.6 %expert_pass.1 = (bf16[768,704]{1,0:T(8,128)(2,1)}, bf16[768,704]{1,0:T(8,128)(2,1)}, bf16[768,704]{1,0:T(8,128)(2,1)}, bf16[768,704]{1,0:T(8,128)(2,1)}, f32[76...) custom-call(s32[4]{0:T(128)} %pad_add_fusion.place_ref, ...), custom_call_target="tpu_custom_call" | custom-call | flops 173015040 | bytes 393216 | tf_op jit(solution)/shard_map/expert_pass/pallas_call | solution.py:292
  218.4 6.6 %all-to-all-start.1 = ((bf16[16,48,1152]{2,1,0:T(8,128)(2,1)}), bf16[16,48,1152]{2,1,0:T(8,128)(2,1)}, u32[]{:S(2)}, u32[]{:S(2)}) async-start(bf16[16,48,1152]{2,1,0:T(8,128)(2,1)} %bitcast.158), calls=%async_computation.1 | async-start | bytes 3538944 | tf_op jit(solution)/shard_map/all_to_all | solution.py:47
  225.0 13.5 %weight_grads.1 = (bf16[96,2048]{1,0:T(8,128)(2,1)}, bf16[96,2048]{1,0:T(8,128)(2,1)}, bf16[96,2048]{1,0:T(8,128)(2,1)}, bf16[96,2048]{1,0:T(8,128)(2,1)}, bf16[...) custom-call(s32[4]{0:T(128)} %pad_add_fusion.place_ref, ...), custom_call_target="tpu_custom_call" | custom-call | flops 103809024 | bytes 294912 | tf_op jit(solution)/shard_map/weight_grads/pallas_call | solution.py:371
  241.3 7.8 %produce.1 = (f32[768,1024]{1,0:T(8,128)}, bf16[768,1024]{1,0:T(8,128)(2,1)}) custom-call(s32[4]{0:T(128)} %pad_add_fusion.place_ref, bf16[768,704]{1,0:T(8,128)(2,1)} %get-tuple-element.141.act_ref, bf16[768,2176]{1,0:T(8,128)(2,1)} %bitcast.19.mine_ref.grad_mine_ref.gate_ref.refs_3_.refs_5_, bf16[4,176,2048]{2,1,0:T(8,128)(2,1)} %own_down.3, ...), custom_call_target="tpu_custom_call" | custom-call | flops 34603008 | bytes 147456 | tf_op jit(solution)/shard_map/produce/pallas_call | solution.py:324
  252.1 5.9 %combine_rows.2 = (bf16[4,48,2176]{2,1,0:T(8,128)(2,1)}, f32[4,48,2176]{2,1,0:T(8,128)}) custom-call(s32[4]{0:T(128)} %pad_add_fusion.place_ref, bf16[768,384]{1,0:T(8,128)(2,1)} %fusion.4.pick_ref, bf16[768,1152]{1,0:T(8,128)(2,1)} %bitcast.23.returned_ref, f32[384,2048]{1,0:T(8,128)} %get-tuple-element.145.shared_ref), custom_call_target="tpu_custom_call" | custom-call | flops 10937500 | bytes 131072 | tf_op jit(solution)/shard_map/combine_rows/pallas_call | solution.py:729
  273.4 6.7 %all-to-all-start.2 = ((bf16[16,48,1024]{2,1,0:T(8,128)(2,1)}), bf16[16,48,1024]{2,1,0:T(8,128)(2,1)}, u32[]{:S(2)}, u32[]{:S(2)}) async-start(bf16[16,48,1024]{2,1,0:T(8,128)(2,1)} %bitcast.159), calls=%async_computation.2 | async-start | bytes 3145728 | tf_op jit(solution)/shard_map/all_to_all | solution.py:47
  290.4 4.4 collective-permute-done.30.refs_3_
  295.4 6.0 %collective-permute-done.28.refs_1_ = bf16[48,2176]{1,0:T(8,128)(2,1)} collective-permute-done((bf16[48,2176]{1,0:T(8,128)(2,1)S(1)}, bf16[48,2176]{1,0:T(8,128)(2,1)}, u32[]{:S(2)}, u32[]{:S(2)}) %collective-permute-start.28) | collective-permute-done | bytes 208928 | tf_op jit(solution)/shard_map/ppermute | solution.py:43
  307.6 18.7 %attention_backward.1 = (bf16[4,4,48,576]{3,2,1,0:T(8,128)(2,1)}, f32[4,4,48,576]{3,2,1,0:T(8,128)}, bf16[1536,512]{1,0:T(8,128)(2,1)}, bf16[384,384]{1,0:T(8,12...) custom-call(s32[4]{0:T(128)} %pad_add_fusion.place_ref, ...), custom_call_target="tpu_custom_call" | custom-call | flops 62500000 | bytes 262144 | tf_op jit(solution)/shard_map/attention_backward/pallas_call | solution.py:652
  339.3 4.5 all-to-all-start.3
  355.6 4.5 all-to-all-done.3
  364.7 5.8 %all-to-all-start.4 = ((bf16[8,48,72]{2,1,0:T(8,128)(2,1)}), bf16[8,48,72]{2,1,0:T(8,128)(2,1)S(1)}, u32[]{:S(2)}, u32[]{:S(2)}) async-start(bf16[8,48,72]{2,1,0:T(8,128)(2,1)} %bitcast.145), calls=%async_computation.4 | async-start | bytes 196608 | tf_op jit(solution)/shard_map/all_to_all | solution.py:1090
  370.5 6.8 %projection_grads.1 = bf16[2048,768]{1,0:T(8,128)(2,1)} custom-call(bf16[384,2048]{1,0:T(8,128)(2,1)} %copy-done.2, bf16[384,2176]{1,0:T(8,128)(2,1)} %get-tuple-element.158.branch, bf16[1536,512]{1,0:T(8,128)(2,1)} %get-tuple-element.154.compressed_ref.compressed, bf16[384,384]{1,0:T(8,128)(2,1)} %get-tuple-element.159.query_grad, ...), custom_call_target="tpu_custom_call" | custom-call | flops 31250000 | bytes 163840 | tf_op jit(solution)/shard_map/projection_grads/pallas_call | solution.py:689
  389.6 4.1 pad_maximum_fusion
  394.3 6.6 %all-to-all-start.5 = ((bf16[16,144,768]{2,1,0:T(8,128)(2,1)}), bf16[16,144,768]{2,1,0:T(8,128)(2,1)}, u32[]{:S(2)}, u32[]{:S(2)}) async-start(bf16[16,144,768]{2,1,0:T(8,128)(2,1)} %pad_maximum_fusion), calls=%async_computation.5 | async-start | bytes 7077888 | tf_op jit(solution)/shard_map/all_to_all | solution.py:47
  402.8 5.7 %combine_rows.3 = (bf16[4,48,2048]{2,1,0:T(8,128)(2,1)}, f32[4,48,2048]{2,1,0:T(8,128)}) custom-call(s32[4]{0:T(128)} %pad_add_fusion.place_ref, bf16[768,384]{1,0:T(8,128)(2,1)} %fusion.4.pick_ref, bf16[768,1024]{1,0:T(8,128)(2,1)} %bitcast.28.returned_ref, f32[384,2048]{1,0:T(8,128)} %get-tuple-element.125.shared_ref), custom_call_target="tpu_custom_call" | custom-call | flops 10937500 | bytes 131072 | tf_op jit(solution)/shard_map/combine_rows/pallas_call | solution.py:729
  419.5 6.1 %collective-permute-done.44 = bf16[48,2048]{1,0:T(8,128)(2,1)S(1)} collective-permute-done((bf16[48,2048]{1,0:T(8,128)(2,1)S(1)}, bf16[48,2048]{1,0:T(8,128)(2,1)S(1)}, u32[]{:S(2)}, u32[]{:S(2)}) %collective-permute-start.44) | collective-permute-done | bytes 196640 | tf_op jit(solution)/shard_map/ppermute | solution.py:43
  425.6 7.9 %collective-permute-done.45 = bf16[48,2048]{1,0:T(8,128)(2,1)} collective-permute-done((bf16[48,2048]{1,0:T(8,128)(2,1)S(1)}, bf16[48,2048]{1,0:T(8,128)(2,1)}, u32[]{:S(2)}, u32[]{:S(2)}) %collective-permute-start.45) | collective-permute-done | bytes 196640 | tf_op jit(solution)/shard_map/ppermute | solution.py:43
  445.2 8.9 %all-to-all-done.5 = bf16[16,144,768]{2,1,0:T(8,128)(2,1)} async-done(((bf16[16,144,768]{2,1,0:T(8,128)(2,1)}), bf16[16,144,768]{2,1,0:T(8,128)(2,1)}, u32[]{:S(2)}, u32[]{:S(2)}) %all-to-all-start.5) | async-done | bytes 3538976 | tf_op jit(solution)/shard_map/all_to_all | solution.py:47
  466.7 23.8 %collective-permute-done.49.refs_15_ = bf16[224,2048]{1,0:T(8,128)(2,1)} collective-permute-done((bf16[224,2048]{1,0:T(8,128)(2,1)}, bf16[224,2048]{1,0:T(8,128)(2,1)}, u32[]{:S(2)}, u32[]{:S(2)}) %collective-permute-start.49) | collective-permute-done | bytes 917536 | tf_op jit(solution)/shard_map/ppermute | solution.py:43
  491.2 3.8 all-to-all-start.6
  499.5 9.8 %unpack_gradients.1 = (f32[4,176,2048]{2,1,0:T(8,128)}, f32[4,176,2048]{2,1,0:T(8,128)}, f32[4,176,2048]{2,1,0:T(8,128)}) custom-call(s32[1]{0:T(128)} %bitcast.x_ref, bf16[96,2048]{1,0:T(8,128)(2,1)} %get-tuple-element.199.refs_0_, bf16[96,2048]{1,0:T(8,128)(2,1)} %copy-done.20, bf16[96,2048]{1,0:T(8,128)(2,1)} %collective-permute-done.22.refs_2_, ...), custom_call_target="tpu_custom_call" | custom-call | bytes 425984 | tf_op jit(solution)/shard_map/unpack_gradients/pallas_call | solution.py:183
  (298 shorter events, 207.2 us)
Async XLA Ops:
  19.3 19.3 %collective-permute-start.1 = (bf16[192,576]{1,0:T(8,128)(2,1)}, bf16[192,576]{1,0:T(8,128)(2,1)}, u32[]{:S(2)}, u32[]{:S(2)}) collective-permute-start(bf16[192,576]{1,0:T(8,128)(2,1)} %get-tuple-element.302), channel_id=1, source_target_pairs={{0,16},{8,24},{16,0},{24,8},{1,17},{9,25},{17,1},{25,9},{2,18},{10... | collective-permute-start | bytes 663560 | tf_op jit(solution)/shard_map/ppermute | solution.py:43
  25.7 38.4 %collective-permute-start.4 = (bf16[208,2048]{1,0:T(8,128)(2,1)}, bf16[208,2048]{1,0:T(8,128)(2,1)}, u32[]{:S(2)}, u32[]{:S(2)}) collective-permute-start(bf16[208,2048]{1,0:T(8,128)(2,1)} %get-tuple-element.118), channel_id=1, source_target_pairs={{0,2},{2,4},{4,6},{6,0},{1,3},{3,5},{5,7},{7,1},{8,10},{10,12},{12... | collective-permute-start | bytes 2555912 | tf_op jit(solution)/shard_map/ppermute | solution.py:43
  26.9 38.5 %collective-permute-start.5 = (bf16[208,2048]{1,0:T(8,128)(2,1)}, bf16[208,2048]{1,0:T(8,128)(2,1)}, u32[]{:S(2)}, u32[]{:S(2)}) collective-permute-start(bf16[208,2048]{1,0:T(8,128)(2,1)} %get-tuple-element.119), channel_id=1, source_target_pairs={{0,4},{2,6},{4,0},{6,2},{1,5},{3,7},{5,1},{7,3},{8,12},{10,14},{12... | collective-permute-start | bytes 2555912 | tf_op jit(solution)/shard_map/ppermute | solution.py:43
  35.0 30.9 %collective-permute-start.6 = (bf16[208,2048]{1,0:T(8,128)(2,1)}, bf16[208,2048]{1,0:T(8,128)(2,1)}, u32[]{:S(2)}, u32[]{:S(2)}) collective-permute-start(bf16[208,2048]{1,0:T(8,128)(2,1)} %get-tuple-element.120), channel_id=1, source_target_pairs={{0,6},{2,0},{4,2},{6,4},{1,7},{3,1},{5,3},{7,5},{8,14},{10,8},{12,... | collective-permute-start | bytes 2555912 | tf_op jit(solution)/shard_map/ppermute | solution.py:43
  115.5 65.1 %all-to-all-start = ((bf16[16,48,2176]{2,1,0:T(8,128)(2,1)}), bf16[16,48,2176]{2,1,0:T(8,128)(2,1)}, u32[]{:S(2)}, u32[]{:S(2)}) async-start(bf16[16,48,2176]{2,1,0:T(8,128)(2,1)} %bitcast.162), calls=%async_computation | async-start | bytes 6684672 | tf_op jit(solution)/shard_map/all_to_all | solution.py:47
  120.7 59.5 %collective-permute-start.15 = (bf16[320,2048]{1,0:T(8,128)(2,1)}, bf16[320,2048]{1,0:T(8,128)(2,1)}, u32[]{:S(2)}, u32[]{:S(2)}) collective-permute-start(bf16[320,2048]{1,0:T(8,128)(2,1)} %get-tuple-element.126), channel_id=1, source_target_pairs={{0,2},{2,4},{4,6},{6,0},{1,3},{3,5},{5,7},{7,1},{8,10},{10,12},{12... | collective-permute-start | bytes 3932168 | tf_op jit(solution)/shard_map/ppermute | solution.py:43
  120.8 59.5 %collective-permute-start.16 = (bf16[320,2048]{1,0:T(8,128)(2,1)}, bf16[320,2048]{1,0:T(8,128)(2,1)}, u32[]{:S(2)}, u32[]{:S(2)}) collective-permute-start(bf16[320,2048]{1,0:T(8,128)(2,1)} %get-tuple-element.128), channel_id=1, source_target_pairs={{0,4},{2,6},{4,0},{6,2},{1,5},{3,7},{5,1},{7,3},{8,12},{10,14},{12... | collective-permute-start | bytes 3932168 | tf_op jit(solution)/shard_map/ppermute | solution.py:43
  122.3 58.2 %collective-permute-start.17 = (bf16[320,2048]{1,0:T(8,128)(2,1)}, bf16[320,2048]{1,0:T(8,128)(2,1)}, u32[]{:S(2)}, u32[]{:S(2)}) collective-permute-start(bf16[320,2048]{1,0:T(8,128)(2,1)} %get-tuple-element.130), channel_id=1, source_target_pairs={{0,6},{2,0},{4,2},{6,4},{1,7},{3,1},{5,3},{7,5},{8,14},{10,8},{12,... | collective-permute-start | bytes 3932168 | tf_op jit(solution)/shard_map/ppermute | solution.py:43
  218.4 33.8 %all-to-all-start.1 = ((bf16[16,48,1152]{2,1,0:T(8,128)(2,1)}), bf16[16,48,1152]{2,1,0:T(8,128)(2,1)}, u32[]{:S(2)}, u32[]{:S(2)}) async-start(bf16[16,48,1152]{2,1,0:T(8,128)(2,1)} %bitcast.158), calls=%async_computation.1 | async-start | bytes 3538944 | tf_op jit(solution)/shard_map/all_to_all | solution.py:47
  225.0 210.5 %reduce-scatter.2.cloned.1.call-start = ((), (), s32[]{:S(2)}) async-start(), calls=%async_computation.10 | async-start | bytes 5013504 | tf_op jit(solution)/shard_map/reduce_scatter | solution.py:1042
  238.5 19.5 %collective-permute-start.21 = (bf16[96,2048]{1,0:T(8,128)(2,1)}, bf16[96,2048]{1,0:T(8,128)(2,1)S(1)}, u32[]{:S(2)}, u32[]{:S(2)}) collective-permute-start(bf16[96,2048]{1,0:T(8,128)(2,1)} %get-tuple-element.148), channel_id=1, source_target_pairs={{0,6},{2,0},{4,2},{6,4},{1,7},{3,1},{5,3},{7,5},{8,14},{10,8},{12,... | collective-permute-start | bytes 1179656 | tf_op jit(solution)/shard_map/ppermute | solution.py:43
  240.6 17.4 %collective-permute-start.22 = (bf16[96,2048]{1,0:T(8,128)(2,1)}, bf16[96,2048]{1,0:T(8,128)(2,1)}, u32[]{:S(2)}, u32[]{:S(2)}) collective-permute-start(bf16[96,2048]{1,0:T(8,128)(2,1)} %get-tuple-element.149), channel_id=1, source_target_pairs={{0,4},{2,6},{4,0},{6,2},{1,5},{3,7},{5,1},{7,3},{8,12},{10,14},{12... | collective-permute-start | bytes 1179656 | tf_op jit(solution)/shard_map/ppermute | solution.py:43
  240.6 20.6 %collective-permute-start.23 = (bf16[96,2048]{1,0:T(8,128)(2,1)}, bf16[96,2048]{1,0:T(8,128)(2,1)}, u32[]{:S(2)}, u32[]{:S(2)}) collective-permute-start(bf16[96,2048]{1,0:T(8,128)(2,1)} %get-tuple-element.150), channel_id=1, source_target_pairs={{0,2},{2,4},{4,6},{6,0},{1,3},{3,5},{5,7},{7,1},{8,10},{10,12},{12... | collective-permute-start | bytes 1179656 | tf_op jit(solution)/shard_map/ppermute | solution.py:43
  273.4 56.1 %all-to-all-start.2 = ((bf16[16,48,1024]{2,1,0:T(8,128)(2,1)}), bf16[16,48,1024]{2,1,0:T(8,128)(2,1)}, u32[]{:S(2)}, u32[]{:S(2)}) async-start(bf16[16,48,1024]{2,1,0:T(8,128)(2,1)} %bitcast.159), calls=%async_computation.2 | async-start | bytes 3145728 | tf_op jit(solution)/shard_map/all_to_all | solution.py:47
  304.5 21.8 %collective-permute-start.32 = (bf16[112,2048]{1,0:T(8,128)(2,1)}, bf16[112,2048]{1,0:T(8,128)(2,1)}, u32[]{:S(2)}, u32[]{:S(2)}) collective-permute-start(bf16[112,2048]{1,0:T(8,128)(2,1)} %get-tuple-element.167), channel_id=1, source_target_pairs={{0,6},{2,0},{4,2},{6,4},{1,7},{3,1},{5,3},{7,5},{8,14},{10,8},{12,... | collective-permute-start | bytes 1376264 | tf_op jit(solution)/shard_map/ppermute | solution.py:43
  305.8 20.5 %collective-permute-start.33 = (bf16[112,2048]{1,0:T(8,128)(2,1)}, bf16[112,2048]{1,0:T(8,128)(2,1)}, u32[]{:S(2)}, u32[]{:S(2)}) collective-permute-start(bf16[112,2048]{1,0:T(8,128)(2,1)} %get-tuple-element.169), channel_id=1, source_target_pairs={{0,4},{2,6},{4,0},{6,2},{1,5},{3,7},{5,1},{7,3},{8,12},{10,14},{12... | collective-permute-start | bytes 1376264 | tf_op jit(solution)/shard_map/ppermute | solution.py:43
  305.9 23.6 %collective-permute-start.34 = (bf16[112,2048]{1,0:T(8,128)(2,1)}, bf16[112,2048]{1,0:T(8,128)(2,1)}, u32[]{:S(2)}, u32[]{:S(2)}) collective-permute-start(bf16[112,2048]{1,0:T(8,128)(2,1)} %get-tuple-element.171), channel_id=1, source_target_pairs={{0,2},{2,4},{4,6},{6,0},{1,3},{3,5},{5,7},{7,1},{8,10},{10,12},{12... | collective-permute-start | bytes 1376264 | tf_op jit(solution)/shard_map/ppermute | solution.py:43
  339.3 20.8 %all-to-all-start.3 = ((bf16[16,48,576]{2,1,0:T(8,128)(2,1)}), bf16[16,48,576]{2,1,0:T(8,128)(2,1)}, u32[]{:S(2)}, u32[]{:S(2)}) async-start(bf16[16,48,576]{2,1,0:T(8,128)(2,1)} %bitcast.161), calls=%async_computation.3 | async-start | bytes 1966080 | tf_op jit(solution)/shard_map/all_to_all | solution.py:1070
  349.1 28.8 %collective-permute-start.37 = (bf16[48,2048]{1,0:T(8,128)(2,1)}, bf16[48,2048]{1,0:T(8,128)(2,1)S(1)}, u32[]{:S(2)}, u32[]{:S(2)}) collective-permute-start(bf16[48,2048]{1,0:T(8,128)(2,1)} %get-tuple-element.309), channel_id=1, source_target_pairs={{0,2},{2,4},{4,6},{6,0},{1,3},{3,5},{5,7},{7,1},{8,10},{10,12},{12... | collective-permute-start | bytes 589832 | tf_op jit(solution)/shard_map/ppermute | solution.py:43
  350.6 28.8 %collective-permute-start.39 = (bf16[48,2048]{1,0:T(8,128)(2,1)}, bf16[48,2048]{1,0:T(8,128)(2,1)S(1)}, u32[]{:S(2)}, u32[]{:S(2)}) collective-permute-start(bf16[48,2048]{1,0:T(8,128)(2,1)} %get-tuple-element.310), channel_id=1, source_target_pairs={{0,6},{2,0},{4,2},{6,4},{1,7},{3,1},{5,3},{7,5},{8,14},{10,8},{12,... | collective-permute-start | bytes 589832 | tf_op jit(solution)/shard_map/ppermute | solution.py:43
  351.9 27.4 %collective-permute-start.38 = (bf16[48,2048]{1,0:T(8,128)(2,1)S(1)}, bf16[48,2048]{1,0:T(8,128)(2,1)}, u32[]{:S(2)}, u32[]{:S(2)}) collective-permute-start(bf16[48,2048]{1,0:T(8,128)(2,1)S(1)} %get-tuple-element.311), channel_id=1, source_target_pairs={{0,4},{2,6},{4,0},{6,2},{1,5},{3,7},{5,1},{7,3},{8,12},{10,14},{12... | collective-permute-start | bytes 589832 | tf_op jit(solution)/shard_map/ppermute | solution.py:43
  353.6 40.7 %collective-permute-start.40 = (bf16[96,2048]{1,0:T(8,128)(2,1)}, bf16[96,2048]{1,0:T(8,128)(2,1)}, u32[]{:S(2)}, u32[]{:S(2)}) collective-permute-start(bf16[96,2048]{1,0:T(8,128)(2,1)} %get-tuple-element.181), channel_id=1, source_target_pairs={{0,6},{2,0},{4,2},{6,4},{1,7},{3,1},{5,3},{7,5},{8,14},{10,8},{12,... | collective-permute-start | bytes 1179656 | tf_op jit(solution)/shard_map/ppermute | solution.py:43
  354.4 39.8 %collective-permute-start.41 = (bf16[96,2048]{1,0:T(8,128)(2,1)}, bf16[96,2048]{1,0:T(8,128)(2,1)}, u32[]{:S(2)}, u32[]{:S(2)}) collective-permute-start(bf16[96,2048]{1,0:T(8,128)(2,1)} %get-tuple-element.183), channel_id=1, source_target_pairs={{0,4},{2,6},{4,0},{6,2},{1,5},{3,7},{5,1},{7,3},{8,12},{10,14},{12... | collective-permute-start | bytes 1179656 | tf_op jit(solution)/shard_map/ppermute | solution.py:43
  364.7 18.6 %all-to-all-start.4 = ((bf16[8,48,72]{2,1,0:T(8,128)(2,1)}), bf16[8,48,72]{2,1,0:T(8,128)(2,1)S(1)}, u32[]{:S(2)}, u32[]{:S(2)}) async-start(bf16[8,48,72]{2,1,0:T(8,128)(2,1)} %bitcast.145), calls=%async_computation.4 | async-start | bytes 196608 | tf_op jit(solution)/shard_map/all_to_all | solution.py:1090
  394.3 59.9 %all-to-all-start.5 = ((bf16[16,144,768]{2,1,0:T(8,128)(2,1)}), bf16[16,144,768]{2,1,0:T(8,128)(2,1)}, u32[]{:S(2)}, u32[]{:S(2)}) async-start(bf16[16,144,768]{2,1,0:T(8,128)(2,1)} %pad_maximum_fusion), calls=%async_computation.5 | async-start | bytes 7077888 | tf_op jit(solution)/shard_map/all_to_all | solution.py:47
  400.9 40.9 %all-gather.5.cloned.1.call-start = ((), (), s32[]{:S(2)}) async-start(), calls=%async_computation.9 | async-start | bytes 1769472 | tf_op jit(solution)/shard_map/all_gather | solution.py:86
  402.8 108.9 %all-gather.3.cloned.1.call-start = ((), (), s32[]{:S(2)}) async-start(), calls=%async_computation.8 | async-start | bytes 1769472 | tf_op jit(solution)/shard_map/all_gather | solution.py:86
  416.9 16.5 %collective-permute-start.45 = (bf16[48,2048]{1,0:T(8,128)(2,1)S(1)}, bf16[48,2048]{1,0:T(8,128)(2,1)}, u32[]{:S(2)}, u32[]{:S(2)}) collective-permute-start(bf16[48,2048]{1,0:T(8,128)(2,1)S(1)} %get-tuple-element.308), channel_id=1, source_target_pairs={{0,4},{2,6},{4,0},{6,2},{1,5},{3,7},{5,1},{7,3},{8,12},{10,14},{12... | collective-permute-start | bytes 589832 | tf_op jit(solution)/shard_map/ppermute | solution.py:43
  439.8 26.9 %collective-permute-start.47 = (bf16[224,2048]{1,0:T(8,128)(2,1)}, bf16[224,2048]{1,0:T(8,128)(2,1)}, u32[]{:S(2)}, u32[]{:S(2)}) collective-permute-start(bf16[224,2048]{1,0:T(8,128)(2,1)} %get-tuple-element.193), channel_id=1, source_target_pairs={{0,6},{2,0},{4,2},{6,4},{1,7},{3,1},{5,3},{7,5},{8,14},{10,8},{12,... | collective-permute-start | bytes 2752520 | tf_op jit(solution)/shard_map/ppermute | solution.py:43
  440.5 26.3 %collective-permute-start.48 = (bf16[224,2048]{1,0:T(8,128)(2,1)}, bf16[224,2048]{1,0:T(8,128)(2,1)}, u32[]{:S(2)}, u32[]{:S(2)}) collective-permute-start(bf16[224,2048]{1,0:T(8,128)(2,1)} %get-tuple-element.195), channel_id=1, source_target_pairs={{0,4},{2,6},{4,0},{6,2},{1,5},{3,7},{5,1},{7,3},{8,12},{10,14},{12... | collective-permute-start | bytes 2752520 | tf_op jit(solution)/shard_map/ppermute | solution.py:43
  441.8 48.8 %collective-permute-start.49 = (bf16[224,2048]{1,0:T(8,128)(2,1)}, bf16[224,2048]{1,0:T(8,128)(2,1)}, u32[]{:S(2)}, u32[]{:S(2)}) collective-permute-start(bf16[224,2048]{1,0:T(8,128)(2,1)} %get-tuple-element.197), channel_id=1, source_target_pairs={{0,2},{2,4},{4,6},{6,0},{1,3},{3,5},{5,7},{7,1},{8,10},{10,12},{12... | collective-permute-start | bytes 2752520 | tf_op jit(solution)/shard_map/ppermute | solution.py:43
  491.2 18.0 %all-to-all-start.6 = ((bf16[8,96,128]{2,1,0:T(8,128)(2,1)}), bf16[8,96,128]{2,1,0:T(8,128)(2,1)S(1)}, u32[]{:S(2)}, u32[]{:S(2)}) async-start(bf16[8,96,128]{2,1,0:T(8,128)(2,1)} %broadcast_in_dim.35), calls=%async_computation.6 | async-start | bytes 393216 | tf_op jit(solution)/shard_map/all_to_all | solution.py:1151
  (67 other events, 484.6 us)
Sparse Core Ops, SparseCore 0:
  262.3 98.1 reduce-scatter.1
Sparse Core Ops, SparseCore 1:
  403.6 28.6 all-gather.4
  435.5 56.5 all-gather.2
